TPU v7x, 256 devices: a whole 4x4x8 slice. The times are simulated.
256 devices in a mesh: dp: 16 (over x_hi, y, core), tensor: 16 (over x_lo, z).
Axes of the slice: x: 4 (x_hi: 2, x_lo: 2; x = x_hi * 2 + x_lo), y: 4, z: 8, core: 2. Of those that a mesh axis runs over, the one named last changes fastest.
Arguments:
- tokens: bfloat16 [4096, 4096], P(('dp', 'tensor')), may hold values from -24 to 24
- gate_weight: bfloat16 [4096, 14336], P('dp', 'tensor'), may hold values from -0.09375 to 0.09375
- up_weight: bfloat16 [4096, 14336], P('dp', 'tensor'), may hold values from -0.09375 to 0.09375
- hidden_cotangent: bfloat16 [4096, 14336], P('dp', 'tensor'), may hold values from -1.5 to 1.5
Outputs:
- hidden: bfloat16 [4096, 14336], P('dp', 'tensor')
- grad_tokens: bfloat16 [4096, 4096], P(('dp', 'tensor'))
- grad_gate: bfloat16 [4096, 14336], P('dp', 'tensor')
- grad_up: bfloat16 [4096, 14336], P('dp', 'tensor')
All inputs are finite; a program needn't handle non-finite values.
Results may differ from a plain program's by a relative error of at most 0.023.
Values may be sent and summed in bfloat16 or wider, within the bound.
A program may use at most 64 MiB of HBM per device.

v0:
```python
import jax
import jax.numpy as jnp
from jax import lax
from jax.sharding import Mesh
from jax.sharding import PartitionSpec as P

TENSOR = ("tensor_0", "tensor_1")
DP_TENSOR = ("dp", "tensor_0", "tensor_1")


def from_everyone(value, axis):
    peers = lax.axis_size(axis)
    return lax.all_to_all(
        jnp.broadcast_to(value[None], (peers, *value.shape)), axis, 0, 0, tiled=True
    )


def joined_along(tiles, dim):
    tiles = jnp.moveaxis(tiles, 0, dim)
    shape = tiles.shape
    return tiles.reshape(*shape[:dim], shape[dim] * shape[dim + 1], *shape[dim + 2 :])


def collect(value, axis, dim):
    tiles = from_everyone(value, axis)
    return joined_along(tiles, dim)


def in_one_piece(arrays, axis, dim, along):
    ends, at = ([], 0)
    for a in arrays[:-1]:
        at += a.shape[along]
        ends.append(at)
    both = jnp.concatenate(arrays, axis=along)
    return tuple(jnp.split(lax.all_gather(both, axis, axis=dim, tiled=True), ends, axis=along))


def own_block(tiles, axes, turns):
    shape = [lax.axis_size(a) for a in axes]
    tiles = tiles.reshape(*shape, *tiles.shape[1:])
    tiles = tiles.transpose(*turns, *range(len(axes), tiles.ndim))
    tiles = tiles.reshape(-1, *tiles.shape[len(axes) :])
    for k in turns:
        tiles = lax.psum_scatter(tiles, axes[k], scatter_dimension=0, tiled=True)
    return tiles[0]


def cut_along(value, dim, peers):
    before, after = (value.shape[:dim], value.shape[dim + 1 :])
    return jnp.moveaxis(value.reshape(*before, peers, -1, *after), dim, 0)


def summed_rows(value, axes, turns, dim):
    peers = lax.axis_size(axes)
    return own_block(cut_along(value, dim, peers), axes, turns)


def swiglu_parts(gate_pre, up_pre, cotangent):
    sigmoid_val = jax.nn.sigmoid(gate_pre)
    activation = gate_pre * sigmoid_val
    hidden = (activation * up_pre).astype(jnp.bfloat16)
    upstream = cotangent.astype(jnp.float32)
    slope = sigmoid_val * (1.0 + gate_pre * (1.0 - sigmoid_val))
    grad_gate_pre = (upstream * up_pre * slope).astype(jnp.bfloat16)
    grad_up_pre = (upstream * activation).astype(jnp.bfloat16)
    return (hidden, grad_gate_pre, grad_up_pre)


def body(tokens, gate_weight, up_weight, hidden_cotangent):
    width = gate_weight.shape[1]
    gathered = collect(tokens, TENSOR, 0)
    full_gate, full_up = in_one_piece((gate_weight, up_weight), "dp", 0, 1)
    gate_pre = jnp.dot(gathered, full_gate, preferred_element_type=jnp.float32)
    up_pre = jnp.dot(gathered, full_up, preferred_element_type=jnp.float32)
    hidden, grad_gate_pre, grad_up_pre = swiglu_parts(gate_pre, up_pre, hidden_cotangent)
    result = jnp.einsum("tf,df->td", grad_gate_pre, full_gate, preferred_element_type=jnp.float32)
    input_rows = summed_rows(
        (
            result
            + jnp.einsum("tf,df->td", grad_up_pre, full_up, preferred_element_type=jnp.float32)
        ).astype(jnp.bfloat16),
        TENSOR,
        (1, 0),
        0,
    ).astype(jnp.float32)
    joined_grad = jnp.concatenate([grad_gate_pre, grad_up_pre], axis=1)
    weight_total = lax.psum_scatter(
        lax.dot_general(
            gathered, joined_grad, (((0,), (0,)), ((), ())), preferred_element_type=jnp.float32
        ).astype(jnp.bfloat16),
        "dp",
        scatter_dimension=0,
        tiled=True,
    ).astype(jnp.float32)
    grad_tokens = input_rows.astype(jnp.bfloat16)
    grad_gate = weight_total[:, :width].astype(jnp.bfloat16)
    grad_up = weight_total[:, width:].astype(jnp.bfloat16)
    return (hidden, grad_tokens, grad_gate, grad_up)


def solution(mesh):
    torus = Mesh(mesh.devices.reshape(mesh.shape["dp"], 2, 8), ("dp", "tensor_0", "tensor_1"))
    in_specs = (P(DP_TENSOR, None), P("dp", TENSOR), P("dp", TENSOR), P("dp", TENSOR))
    out_specs = (P("dp", TENSOR), P(DP_TENSOR, None), P("dp", TENSOR), P("dp", TENSOR))
    return jax.shard_map(body, mesh=torus, in_specs=in_specs, out_specs=out_specs, check_vma=False)
```

profile of v0, /device:TPU:1, one launch (start us, length us, event | category | flops | bytes accessed | tf_op | source)
XLA Modules:
  0.0 353.9 jit_solution(10433681141637652433)
XLA Ops:
  7.2 0.0 copy-start
  7.2 0.0 all-gather.2.cloned.1.call-start
  7.2 2.2 pad_maximum_fusion
  9.4 0.0 all-gather.2.cloned.1.call-update
  9.4 2.4 broadcast_in_dim.2
  11.9 10.0 %all-to-all-start = ((bf16[16,16,4096]{2,1,0:T(8,128)(2,1)}), bf16[16,16,4096]{2,1,0:T(8,128)(2,1)S(1)}, u32[]{:S(2)}, u32[]{:S(2)}) async-start(bf16[16,16,4096]{2,1,0:T(8,128)(2,1)} %broadcast_in_dim.2), calls=%async_computation | async-start | bytes 4194304 | tf_op jit(solution)/shard_map/all_to_all | solution.py:13
  21.9 0.0 reduce-scatter.4.cloned.1.call-start
  22.0 0.2 copy.8
  22.2 47.3 %all-to-all-done = bf16[16,16,4096]{2,1,0:T(8,128)(2,1)S(1)} async-done(((bf16[16,16,4096]{2,1,0:T(8,128)(2,1)}), bf16[16,16,4096]{2,1,0:T(8,128)(2,1)S(1)}, u32[]{:S(2)}, u32[]{:S(2)}) %all-to-all-start) | async-done | bytes 2097184 | tf_op jit(solution)/shard_map/all_to_all | solution.py:13
  69.6 58.3 %all-gather.2.cloned.1.call-done = bf16[4096,1792]{1,0:T(8,128)(2,1)} async-done(((bf16[256,1792]{1,0:T(8,128)(2,1)}), bf16[4096,1792]{1,0:T(8,128)(2,1)}) %all-gather.2.cloned.1.call-update) | async-done | bytes 14680080 | tf_op jit(solution)/shard_map/all_gather | solution.py:35
  127.8 5.3 %fusion.15 = f32[256,896]{0,1:T(8,128)S(1)} fusion(bf16[256,4096]{1,0:T(8,128)(2,1)S(1)} %bitcast.17, bf16[4096,1792]{1,0:T(8,128)(2,1)} %all-gather.2.cloned.1.call-done), kind=kOutput, calls=%fused_computation.12 | convolution fusion | flops 1879048192 | bytes 10354688 | tf_op jit(solution)/shard_map/dot_general | solution.py:73
  133.2 1.9 copy-done.3
  135.1 2.4 fusion.22
  137.5 0.0 copy-start.1
  137.5 4.3 %fusion.1 = f32[256,4096]{1,0:T(8,128)} fusion(bf16[256,896]{0,1:T(8,128)(2,1)S(1)} %get-tuple-element.10, bf16[4096,1792]{1,0:T(8,128)(2,1)S(1)} %copy-done.3), kind=kOutput, calls=%fused_computation.2 | convolution fusion | flops 1879048192 | bytes 11993088 | tf_op jit(solution)/shard_map/tf,df->td/dot_general | solution.py:80
  141.8 0.0 copy-done.1
  141.8 4.6 %fusion.12 = bf16[256,4096]{1,0:T(8,128)(2,1)S(1)} fusion(f32[256,4096]{1,0:T(8,128)} %fusion.1, bf16[256,896]{0,1:T(8,128)(2,1)S(1)} %get-tuple-element.8, bf16[4096,1792]{1,0:T(8,128)(2,1)S(1)} %copy-done.3), kind=kOutput, calls=%fused_computation.11 | convolution fusion | flops 1881145344 | bytes 14090240 | tf_op jit(solution)/shard_map/tf,df->td/dot_general | solution.py:76
  146.5 0.0 copy-start.2
  146.5 1.5 copy.9
  148.0 0.0 reduce-scatter.4.cloned.1.call-update
  148.0 0.2 reduce-scatter.8.cloned.1.call-start
  148.3 8.3 %fusion = bf16[4096,1792]{0,1:T(8,128)(2,1)} fusion(bf16[256,4096]{1,0:T(8,128)(2,1)S(1)} %bitcast.19, bf16[256,896]{0,1:T(8,128)(2,1)S(1)} %copy-done.2, bf16[256,896]{0,1:T(8,128)(2,1)S(1)} %get-tuple-element.8), kind=kOutput, calls=%fused_computation.1 | convolution fusion | flops 3767271424 | bytes 17694720 | tf_op jit(solution)/shard_map/dot_general | solution.py:88
  156.6 0.0 reduce-scatter.8.cloned.1.call-update
  156.6 0.0 reduce-scatter.6.cloned.1.call-start
  156.7 25.3 %reduce-scatter.4.cloned.1.call-done = bf16[2,16,4096]{2,1,0:T(8,128)(2,1)} async-done(((bf16[16,16,4096]{2,1,0:T(8,128)(2,1)}), bf16[2,16,4096]{2,1,0:T(8,128)(2,1)}) %reduce-scatter.4.cloned.1.call-update) | async-done | bytes 262160 | tf_op jit(solution)/shard_map/reduce_scatter | solution.py:44
  182.0 0.0 reduce-scatter.6.cloned.1.call-update
  182.0 1.0 copy.10
  183.0 146.0 %reduce-scatter.8.cloned.1.call-done = bf16[256,1792]{0,1:T(8,128)(2,1)} async-done(((bf16[4096,1792]{0,1:T(8,128)(2,1)}), bf16[256,1792]{0,1:T(8,128)(2,1)}) %reduce-scatter.8.cloned.1.call-update) | async-done | bytes 917520 | tf_op jit(solution)/shard_map/reduce_scatter | solution.py:87
  329.0 1.2 fusion.29
  330.2 1.0 copy.12
  331.2 1.0 copy.11
  332.2 15.2 %reduce-scatter.6.cloned.1.call-done = bf16[1,16,4096]{2,1,0:T(8,128)(2,1)} async-done(((bf16[2,16,4096]{2,1,0:T(8,128)(2,1)}), bf16[1,16,4096]{2,1,0:T(8,128)(2,1)}) %reduce-scatter.6.cloned.1.call-update) | async-done | bytes 131088 | tf_op jit(solution)/shard_map/reduce_scatter | solution.py:44
  (3 shorter events, 0.0 us)
Async XLA Ops:
  7.2 14.8 %copy-start = (bf16[256,896]{1,0:T(8,128)(2,1)S(1)}, bf16[256,896]{1,0:T(8,128)(2,1)}, u32[]{:S(2)}) copy-start(bf16[256,896]{1,0:T(8,128)(2,1)} %param.7) | copy-start | bytes 1376260
  7.2 120.6 %all-gather.2.cloned.1.call-start = ((), (), s32[]{:S(2)}) async-start(), calls=%async_computation.4 | async-start | bytes 15597568 | tf_op jit(solution)/shard_map/all_gather | solution.py:35
  11.9 57.7 %all-to-all-start = ((bf16[16,16,4096]{2,1,0:T(8,128)(2,1)}), bf16[16,16,4096]{2,1,0:T(8,128)(2,1)S(1)}, u32[]{:S(2)}, u32[]{:S(2)}) async-start(bf16[16,16,4096]{2,1,0:T(8,128)(2,1)} %broadcast_in_dim.2), calls=%async_computation | async-start | bytes 4194304 | tf_op jit(solution)/shard_map/all_to_all | solution.py:13
  21.9 160.1 %reduce-scatter.4.cloned.1.call-start = ((), (), s32[]{:S(2)}) async-start(), calls=%async_computation.5 | async-start | bytes 2359296 | tf_op jit(solution)/shard_map/reduce_scatter | solution.py:44
  127.8 7.3 %copy-start.3 = (bf16[4096,1792]{1,0:T(8,128)(2,1)S(1)}, bf16[4096,1792]{1,0:T(8,128)(2,1)}, u32[]{:S(2)}) copy-start(bf16[4096,1792]{1,0:T(8,128)(2,1)} %all-gather.2.cloned.1.call-done) | copy-start | bytes 44040196
  137.5 4.4 %copy-start.1 = (bf16[256,896]{0,1:T(8,128)(2,1)}, bf16[256,896]{0,1:T(8,128)(2,1)S(1)}, u32[]{:S(2)}) copy-start(bf16[256,896]{0,1:T(8,128)(2,1)S(1)} %get-tuple-element.10) | copy-start | bytes 1376260
  146.5 1.8 copy-start.2
  148.0 181.0 %reduce-scatter.8.cloned.1.call-start = ((), (), s32[]{:S(2)}) async-start(), calls=%async_computation.7 | async-start | bytes 15597568 | tf_op jit(solution)/shard_map/reduce_scatter | solution.py:87
  156.6 190.8 %reduce-scatter.6.cloned.1.call-start = ((), (), s32[]{:S(2)}) async-start(), calls=%async_computation.6 | async-start | bytes 393216 | tf_op jit(solution)/shard_map/reduce_scatter | solution.py:44
Sparse Core Ops, SparseCore 0:
  10.8 116.9 all-gather.1
  148.2 33.8 reduce-scatter.3
  186.6 142.3 reduce-scatter.7
  331.9 15.4 reduce-scatter.5
where the time goes:
time: 354 us
  waiting for transfers between devices  292 us (82%)
  matrix products  25 us (7%)
  between operations  13.8 us (4%)
  starting transfers between devices  10.4 us (3%)
  local copies, waits for them, and re-layouts  10.2 us (3%)
    reduce_scatter x1, waiting for transfers between devices, body(): lax.psum_scatter(lax.dot_general(gathered, joined_grad, (((0,), (0,)), ((...  146 us
    all_gather x1, waiting for transfers between devices, in_one_piece(): lax.all_gather(both, axis, axis=dim, tiled=True)  58.3 us
    all_to_all x1, waiting for transfers between devices, from_everyone(): lax.all_to_all(jnp.broadcast_to(value[None], (peers, *value.shape)), axis...  47.3 us
    reduce_scatter x2, waiting for transfers between devices, own_block(): tiles = lax.psum_scatter(tiles, axes[k], scatter_dimension=0, tiled=True)  40.6 us
    all_to_all x1, starting transfers between devices, from_everyone(): lax.all_to_all(jnp.broadcast_to(value[None], (peers, *value.shape)), axis...  10 us
    dot_general x1, matrix products, body(): lax.dot_general(gathered, joined_grad, (((0,), (0,)), ((), ())), preferre...  8.31 us
  transfers between devices with their start and end apart: 5, of which 5 were waited for; matrix products, arithmetic and copies ran while one was open for 4% of the time, Pallas kernels for 0%

commit v1 on v0

v1 whole, which is shorter than its diff:
```python
import jax
import jax.numpy as jnp
from jax import lax
from jax.sharding import Mesh
from jax.sharding import PartitionSpec as P

SPLIT = ("xh", "c")
TENSOR = ("xl", "z")
DP = ("xh", "y", "c")
ROWS = P((*DP, *TENSOR), None)
BLOCK = P(DP, TENSOR)


def swiglu_parts(gate_pre, up_pre, cotangent):
    sigmoid_val = jax.nn.sigmoid(gate_pre)
    activation = gate_pre * sigmoid_val
    hidden = (activation * up_pre).astype(jnp.bfloat16)
    upstream = cotangent.astype(jnp.float32)
    slope = sigmoid_val * (1.0 + gate_pre * (1.0 - sigmoid_val))
    grad_gate_pre = (upstream * up_pre * slope).astype(jnp.bfloat16)
    grad_up_pre = (upstream * activation).astype(jnp.bfloat16)
    return (hidden, grad_gate_pre, grad_up_pre)


def body(tokens, gate_weight, up_weight, cotangent):
    rows, model = tokens.shape
    depth, width = gate_weight.shape
    nx, ny, nc = (lax.axis_size(a) for a in DP)
    nt = lax.axis_size(TENSOR)
    cut = tokens.reshape(rows, nx, ny, nc, depth).transpose(1, 3, 0, 2, 4)
    cut = cut.reshape(nx * nc, rows, ny * depth)
    cut = lax.all_to_all(cut, SPLIT, 0, 0, tiled=True)
    mine = lax.all_gather(cut, TENSOR, axis=1, tiled=True)
    mine = mine.reshape(nx * nc * nt * rows, ny * depth)
    weights = lax.all_gather(
        jnp.concatenate([gate_weight, up_weight], axis=1), "y", axis=0, tiled=True
    )
    part = jnp.dot(mine, weights, preferred_element_type=jnp.float32).astype(jnp.bfloat16)
    pre = lax.psum_scatter(part, SPLIT, scatter_dimension=0, tiled=True).astype(jnp.float32)
    hidden, grad_gate_pre, grad_up_pre = swiglu_parts(pre[:, :width], pre[:, width:], cotangent)
    grads = lax.all_gather(
        jnp.concatenate([grad_gate_pre, grad_up_pre], axis=1), SPLIT, axis=0, tiled=True
    )
    back = lax.dot_general(
        grads, weights, (((1,), (1,)), ((), ())), preferred_element_type=jnp.float32
    ).astype(jnp.bfloat16)
    nl, nz = (lax.axis_size(a) for a in TENSOR)
    back = back.reshape(nx * nc, nl, nz, rows, ny * depth).transpose(2, 1, 0, 3, 4)
    back = lax.psum_scatter(back, "z", scatter_dimension=0, tiled=True)[0]
    back = lax.psum_scatter(back, "xl", scatter_dimension=0, tiled=True)[0]
    back = lax.all_to_all(back, SPLIT, 0, 0, tiled=True)
    back = back.reshape(nx, nc, rows, ny, depth).transpose(2, 0, 3, 1, 4).reshape(rows, model)
    total = lax.dot_general(
        mine, grads, (((0,), (0,)), ((), ())), preferred_element_type=jnp.float32
    ).astype(jnp.bfloat16)
    total = lax.psum_scatter(total, "y", scatter_dimension=0, tiled=True)
    return (hidden, back, total[:, :width], total[:, width:])


def solution(mesh):
    torus = Mesh(mesh.devices.reshape(2, 4, 2, 2, 8), (*DP, *TENSOR))
    specs = (ROWS, BLOCK, BLOCK, BLOCK)
    outs = (BLOCK, ROWS, BLOCK, BLOCK)
    return jax.shard_map(body, mesh=torus, in_specs=specs, out_specs=outs, check_vma=False)
```

time: 354 us -> 427 us (1.21)
  waiting for transfers between devices: 292 us -> 352 us
  blocking collectives: 0 us -> 11.4 us
  starting transfers between devices: 10.4 us -> 5.55 us
    unnamed x4 -> x9, waiting for transfers between devices: 0.07 us -> 106 us
    reduce_scatter x3 -> x2, waiting for transfers between devices: 187 us -> 88.3 us  [the longest x1 52.5 us: body(): lax.psum_scatter(part, SPLIT, scatter_dimension=0, tiled=True)]
    all_gather x1 -> x3, waiting for transfers between devices: 58.3 us -> 154 us  [the longest x1 60.2 us: body(): mine = lax.all_gather(cut, TENSOR, axis=1, tiled=True)]
    all_to_all x1, waiting for transfers between devices: 47.3 us -> 4.13 us  [body(): back = lax.all_to_all(back, SPLIT, 0, 0, tiled=True)]
    all_to_all x0 -> x1, blocking collectives: none -> 11.4 us  [body(): cut = lax.all_to_all(cut, SPLIT, 0, 0, tiled=True)]
    all_to_all x1, starting transfers between devices: 10 us -> 5.08 us  [body(): back = lax.all_to_all(back, SPLIT, 0, 0, tiled=True)]
    squeeze x0 -> x2, local copies, waits for them, and re-layouts: none -> 4.54 us  [the longest x1 2.32 us: body(): back = lax.psum_scatter(back, 'z', scatter_dimension=0, tiled=True)[0]]
    dot_general x5 -> x3, matrix products: 25 us -> 24.7 us  [the longest x1 8.59 us: body(): jnp.dot(mine, weights, preferred_element_type=jnp.float32)]
  transfers between devices with their start and end apart: 5 -> 8, of which waited for: 5 -> 8; matrix products, arithmetic and copies ran while one was open for 4% -> 4% of each run, Pallas kernels for 0% -> 0%
where the time goes in v1:
time: 427 us
  waiting for transfers between devices  352 us (82%)
  matrix products  24.7 us (6%)
  between operations  14.2 us (3%)
  local copies, waits for them, and re-layouts  13.7 us (3%)
  blocking collectives  11.4 us (3%)
  starting transfers between devices  5.55 us (1%)
  other arithmetic  5.14 us (1%)
    unnamed x9, waiting for transfers between devices  106 us
    all_gather x1, waiting for transfers between devices, body(): mine = lax.all_gather(cut, TENSOR, axis=1, tiled=True)  60.2 us
    all_gather x1, waiting for transfers between devices, body(): lax.all_gather(jnp.concatenate([gate_weight, up_weight], axis=1), 'y', ax...  55.2 us
    reduce_scatter x1, waiting for transfers between devices, body(): lax.psum_scatter(part, SPLIT, scatter_dimension=0, tiled=True)  52.5 us
    all_gather x1, waiting for transfers between devices, body(): lax.all_gather(jnp.concatenate([grad_gate_pre, grad_up_pre], axis=1), SPL...  38.6 us
    reduce_scatter x1, waiting for transfers between devices, body(): total = lax.psum_scatter(total, 'y', scatter_dimension=0, tiled=True)  35.8 us
    all_to_all x1, blocking collectives, body(): cut = lax.all_to_all(cut, SPLIT, 0, 0, tiled=True)  11.4 us
    dot_general x1, matrix products, body(): jnp.dot(mine, weights, preferred_element_type=jnp.float32)  8.59 us
  transfers between devices with their start and end apart: 8, of which 8 were waited for; matrix products, arithmetic and copies ran while one was open for 4% of the time, Pallas kernels for 0%

profile of v1, /device:TPU:1, one launch (start us, length us, event | category | flops | bytes accessed | tf_op | source)
XLA Modules:
  0.0 426.6 jit_solution(17104382645673480068)
XLA Ops:
  7.2 1.0 reshape.26
  8.3 11.4 %all_to_all.10 = bf16[4,16,1024]{2,1,0:T(8,128)(2,1)} all-to-all(bf16[4,16,1024]{2,1,0:T(8,128)(2,1)S(1)} %reshape.27), channel_id=1, replica_groups=mesh['xh'=2,'y'=4,'c'=2,'xl'=2,'z'=8] {'xh','c'}, dimensions={0} | all-to-all | bytes 262144 | tf_op jit(solution)/shard_map/all_to_all | solution.py:32
  19.8 2.2 pad_maximum_fusion
  22.0 60.2 %all-gather.6.cloned.1.call-done = bf16[4,256,1024]{2,1,0:T(8,128)(2,1)} async-done(((bf16[4,16,1024]{2,1,0:T(8,128)(2,1)}), bf16[4,256,1024]{2,1,0:T(8,128)(2,1)}) %all-gather.6.cloned.1.call-update) | async-done | bytes 2097168 | tf_op jit(solution)/shard_map/all_gather | solution.py:33
  82.2 55.2 %all-gather.4.cloned.1.call-done = bf16[1024,1792]{1,0:T(8,128)(2,1)} async-done(((bf16[256,1792]{1,0:T(8,128)(2,1)}), bf16[1024,1792]{1,0:T(8,128)(2,1)}) %all-gather.4.cloned.1.call-update) | async-done | bytes 3670032 | tf_op jit(solution)/shard_map/all_gather | solution.py:35
  137.4 8.6 %fusion = bf16[1024,1792]{0,1:T(8,128)(2,1)} fusion(bf16[1024,1792]{1,0:T(8,128)(2,1)} %all-gather.4.cloned.1.call-done, bf16[1024,1024]{1,0:T(8,128)(2,1)} %bitcast.41), kind=kOutput, calls=%fused_computation.2 | convolution fusion | flops 3759931392 | bytes 9437184 | tf_op jit(solution)/shard_map/dot_general | solution.py:38
  146.0 0.9 copy-done
  147.0 0.2 copy.20
  147.2 52.5 %reduce-scatter.9.cloned.1.call-done = bf16[256,1792]{0,1:T(8,128)(2,1)} async-done(((bf16[1024,1792]{0,1:T(8,128)(2,1)}), bf16[256,1792]{0,1:T(8,128)(2,1)}) %reduce-scatter.9.cloned.1.call-update) | async-done | bytes 917520 | tf_op jit(solution)/shard_map/reduce_scatter | solution.py:39
  199.7 1.3 convert_element_type.32
  201.0 0.7 fusion.3
  201.7 1.0 pad_maximum_fusion.1
  202.7 38.6 %all-gather.8.cloned.1.call-done = bf16[1024,1792]{0,1:T(8,128)(2,1)} async-done(((bf16[256,1792]{0,1:T(8,128)(2,1)}), bf16[1024,1792]{0,1:T(8,128)(2,1)}) %all-gather.8.cloned.1.call-update) | async-done | bytes 3670032 | tf_op jit(solution)/shard_map/all_gather | solution.py:41
  241.3 8.5 %convolution_convert_fusion.2 = bf16[1024,1024]{1,0:T(8,128)(2,1)} fusion(bf16[1024,1792]{0,1:T(8,128)(2,1)} %all-gather.8.cloned.1.call-done, bf16[1024,1792]{1,0:T(8,128)(2,1)} %all-gather.4.cloned.1.call-done), kind=kOutput, calls=%fused_computation.4 | convolution fusion | flops 3759144960 | bytes 9437184 | tf_op jit(solution)/shard_map/dot_general | solution.py:44
  249.9 0.6 dynamic-slice
  250.5 77.4 %all-reduce.5.cloned.1.call-done = bf16[8,2,4,16,1024]{4,3,0,1,2:T(8,128)(2,1)} async-done(((bf16[8,2,4,16,1024]{4,3,0,1,2:T(8,128)(2,1)}), bf16[8,2,4,16,1024]{4,3,0,1,2:T(8,128)(2,1)}) %all-reduce.5.cloned.1.call-update) | async-done | bytes 2097168
  327.9 2.3 dynamic-slice_bitcast_fusion
  330.2 0.2 reduce-scatter.11.cloned.1.call-start
  330.5 7.6 %fusion.1 = bf16[1024,1792]{0,1:T(8,128)(2,1)} fusion(bf16[1024,1792]{0,1:T(8,128)(2,1)} %all-gather.8.cloned.1.call-done, bf16[1024,1024]{1,0:T(8,128)(2,1)S(1)} %bitcast.42), kind=kOutput, calls=%fused_computation.3 | convolution fusion | flops 3759931392 | bytes 9437184 | tf_op jit(solution)/shard_map/dot_general | solution.py:53
  338.1 0.7 copy-done.2
  338.7 0.6 dynamic-slice.2
  339.3 28.0 %all-reduce.7.cloned.1.call-done = bf16[2,4,16,1024]{3,2,0,1:T(8,128)(2,1)} async-done(((bf16[2,4,16,1024]{3,2,0,1:T(8,128)(2,1)}), bf16[2,4,16,1024]{3,2,0,1:T(8,128)(2,1)}) %all-reduce.7.cloned.1.call-update) | async-done | bytes 262160
  367.3 2.2 dynamic-slice_bitcast_fusion.1
  369.6 5.1 %all-to-all-start.1 = ((bf16[4,16,1024]{2,1,0:T(8,128)(2,1)}), bf16[4,16,1024]{2,1,0:T(8,128)(2,1)S(1)}, u32[]{:S(2)}, u32[]{:S(2)}) async-start(bf16[4,16,1024]{2,1,0:T(8,128)(2,1)} %dynamic-slice_bitcast_fusion.1), calls=%async_computation.2 | async-start | bytes 262144 | tf_op jit(solution)/shard_map/all_to_all | solution.py:51
  374.6 1.0 copy.22
  375.6 4.1 all-to-all-done.1
  379.8 0.1 copy.21
  380.0 0.7 reshape.31
  380.7 35.8 %reduce-scatter.11.cloned.1.call-done = bf16[256,1792]{0,1:T(8,128)(2,1)} async-done(((bf16[1024,1792]{0,1:T(8,128)(2,1)}), bf16[256,1792]{0,1:T(8,128)(2,1)}) %reduce-scatter.11.cloned.1.call-update) | async-done | bytes 917520 | tf_op jit(solution)/shard_map/reduce_scatter | solution.py:56
  416.5 1.2 fusion.6
  417.8 1.0 copy.23
  418.7 1.0 copy.24
  (22 shorter events, 0.6 us)
Async XLA Ops:
  7.2 75.0 %all-gather.6.cloned.1.call-start = ((), (), s32[]{:S(2)}) async-start(), calls=%async_computation.5 | async-start | bytes 2228224 | tf_op jit(solution)/shard_map/all_gather | solution.py:33
  19.7 117.6 %all-gather.4.cloned.1.call-start = ((), (), s32[]{:S(2)}) async-start(), calls=%async_computation.4 | async-start | bytes 4587520 | tf_op jit(solution)/shard_map/all_gather | solution.py:35
  22.0 177.7 %reduce-scatter.9.cloned.1.call-start = ((), (), s32[]{:S(2)}) async-start(), calls=%async_computation.6 | async-start | bytes 4587520 | tf_op jit(solution)/shard_map/reduce_scatter | solution.py:39
  146.0 1.0 copy-start
  146.0 95.3 %all-gather.8.cloned.1.call-start = ((), (), s32[]{:S(2)}) async-start(), calls=%async_computation.7 | async-start | bytes 4587520 | tf_op jit(solution)/shard_map/all_gather | solution.py:41
  202.7 47.2 %copy-start.3 = (u32[256]{0:T(256)S(1)}, u32[256]{0:T(256)}, u32[]{:S(2)}) copy-start(u32[256]{0:T(256)} %constant.5) | copy-start | bytes 3076
  202.7 127.8 %copy-start.1 = (bf16[4,256,1024]{2,1,0:T(8,128)(2,1)S(1)}, bf16[4,256,1024]{2,1,0:T(8,128)(2,1)}, u32[]{:S(2)}) copy-start(bf16[4,256,1024]{2,1,0:T(8,128)(2,1)} %all-gather.6.cloned.1.call-done) | copy-start | bytes 6291460
  202.7 125.2 %all-reduce.5.cloned.1.call-start = ((), (), s32[]{:S(2)}) async-start(), calls=%async_computation.9 | async-start | bytes 4194304
  249.8 117.5 %all-reduce.7.cloned.1.call-start = ((), (), s32[]{:S(2)}) async-start(), calls=%async_computation.10 | async-start | bytes 524288
  330.2 86.3 %reduce-scatter.11.cloned.1.call-start = ((), (), s32[]{:S(2)}) async-start(), calls=%async_computation.8 | async-start | bytes 4587520 | tf_op jit(solution)/shard_map/reduce_scatter | solution.py:56
  338.0 0.7 copy-start.2
  369.6 10.2 %all-to-all-start.1 = ((bf16[4,16,1024]{2,1,0:T(8,128)(2,1)}), bf16[4,16,1024]{2,1,0:T(8,128)(2,1)S(1)}, u32[]{:S(2)}, u32[]{:S(2)}) async-start(bf16[4,16,1024]{2,1,0:T(8,128)(2,1)} %dynamic-slice_bitcast_fusion.1), calls=%async_computation.2 | async-start | bytes 262144 | tf_op jit(solution)/shard_map/all_to_all | solution.py:51
Sparse Core Ops, SparseCore 0:
  19.9 62.2 all-gather.5
  84.0 53.2 all-gather.3
  146.1 53.5 reduce-scatter.8
  202.8 38.4 all-gather.7
  249.9 77.8 all-reduce.4
  331.0 36.2 all-reduce.6
  369.9 46.6 reduce-scatter.10

commit v2 on v1

v2 whole, which is shorter than its diff:
```python
import functools

import jax
import jax.numpy as jnp
from jax import lax
from jax.experimental import pallas as pl
from jax.experimental.pallas import tpu as pltpu
from jax.sharding import Mesh
from jax.sharding import PartitionSpec as P

SPLIT = ("xh", "c")
TENSOR = ("xl", "z")
DP = ("xh", "y", "c")
ROWS = P((*DP, *TENSOR), None)
BLOCK = P(DP, TENSOR)
MESH = pl.DeviceIdType.MESH
F32 = jnp.float32
BF16 = jnp.bfloat16
CHUNKS = ((0, 512), (512, 384))
NZ = 8
TILE = 256
CUBE = tuple((a, b, d) for a in range(2) for b in range(2) for d in range(2))
STEPS = 4


def dot(a, b):
    return jnp.dot(a, b, preferred_element_type=F32)


def dot_nt(a, b):
    return lax.dot_general(a, b, (((1,), (1,)), ((), ())), preferred_element_type=F32)


def kernel(
    tokens, gate, up, cot, hidden, rows_out, grad_gate, grad_up,
    x, xt, w0, w1, pc0, pc1, rc0, rc1, px0, px1, rx0, rx1, po0, po1, g0, g1, dw0, dw1,
    ry0, ry1, qy0, qy1, dx, zs, zr, ts, tr, loc, cs, cr, zgs, zgr, ws, wr, ms, mr, ys, yr, zrs, zrr, fs, fr,
):
    xh, y, c, xl, z = (lax.axis_index(a) for a in ("xh", "y", "c", "xl", "z"))
    yp, ym, y2 = lax.rem(y + 1, 4), lax.rem(y + 3, 4), lax.rem(y + 2, 4)
    zp, zm = lax.rem(z + 1, NZ), lax.rem(z + NZ - 1, NZ)
    W, PC, RC, PX, RX, PO = (w0, w1), (pc0, pc1), (rc0, rc1), (px0, px1), (rx0, rx1), (po0, po1)
    G, DW, RY, QY = (g0, g1), (dw0, dw1), (ry0, ry1), (qy0, qy1)
    both = range(len(CHUNKS))
    sent = []

    def go(src, dst, send, recv, to):
        copy = pltpu.make_async_remote_copy(
            src_ref=src, dst_ref=dst, send_sem=send, recv_sem=recv,
            device_id=to, device_id_type=MESH,
        )
        copy.start()
        sent.append(copy)
        return copy

    def flip(a, b, d):
        return (
            1 - xh if a else xh,
            1 - c if b else c,
            1 - xl if d else xl,
        )

    def cube_id(a, b, d):
        px, pc, plo = flip(a, b, d)
        return {"xh": px, "c": pc, "xl": plo}

    local = []
    for k, (at, wide) in enumerate(CHUNKS):
        local.append(pltpu.make_async_copy(gate.at[:, pl.ds(at, wide)], W[k].at[y, :, pl.ds(0, wide)], loc.at[2 * k]))
        local.append(pltpu.make_async_copy(up.at[:, pl.ds(at, wide)], W[k].at[y, :, pl.ds(wide, wide)], loc.at[2 * k + 1]))
    own = pltpu.make_async_copy(tokens.at[2 * xh + c], x.at[2 * xh + c, xl, z], loc.at[4])
    for copy in (own, *local):
        copy.start()

    barrier = pltpu.get_barrier_semaphore()
    peers = [{"y": yp}, {"y": ym}, {"z": zp}, {"z": zm}] + [cube_id(*k) for k in CUBE[1:]]
    for peer in peers:
        pl.semaphore_signal(barrier, inc=1, device_id=peer, device_id_type=MESH)
    pl.semaphore_wait(barrier, len(peers))

    cube = []
    for k, key in enumerate(CUBE):
        if k:
            a, b, _ = flip(*key)
            cube.append(go(tokens.at[2 * a + b], x.at[2 * xh + c, xl, z], cs.at[k - 1], cr.at[k - 1], cube_id(*key)))

    def send_weights(k):
        return (
            go(W[k].at[y], W[k].at[y], ws.at[k, 0], wr.at[k, 0], {"y": yp}),
            go(W[k].at[y], W[k].at[y], ws.at[k, 1], wr.at[k, 1], {"y": ym}),
        )

    def relay_weights(k):
        return (
            go(W[k].at[ym, pl.ds(0, 128)], W[k].at[ym, pl.ds(0, 128)], ws.at[k, 2], wr.at[k, 2], {"y": yp}),
            go(W[k].at[yp, pl.ds(128, 128)], W[k].at[yp, pl.ds(128, 128)], ws.at[k, 3], wr.at[k, 3], {"y": ym}),
        )

    for copy in local:
        copy.wait()
    first = send_weights(0)
    own.wait()
    for copy in cube:
        copy.wait_recv()

    def part(at, h):
        return x.at[pl.ds(2 * h, 2), :, at]

    def z_step(step):
        out = []
        for h in range(2):
            if step < 3 or h == 0:
                at = lax.rem(z + NZ - step, NZ)
                out.append(go(part(at, h), part(at, h), zgs.at[step, h, 0], zgr.at[step, h, 0], {"z": zp}))
            if step < 3 or h == 1:
                at = lax.rem(z + step, NZ)
                out.append(go(part(at, h), part(at, h), zgs.at[step, h, 1], zgr.at[step, h, 1], {"z": zm}))
        return out

    def arrived(copies):
        for copy in copies:
            copy.wait_recv()

    moving = z_step(0)
    arrived(moving)
    moving = z_step(1)
    arrived(first)
    relay0 = relay_weights(0)
    second = send_weights(1)
    arrived(moving)
    moving = z_step(2)
    arrived(moving)
    moving = z_step(3)
    arrived(second)
    relay1 = relay_weights(1)
    arrived(moving)
    arrived(relay0)

    def block(ref, at):
        return ref[at].reshape(256, 1024)

    def columns(j):
        return pl.ds(pl.multiple_of(j * TILE, TILE), TILE)

    def partial(k, at, store):
        def step(j, _):
            cols = columns(j)
            store(cols, dot(block(x, at), W[k][:, :, cols].reshape(1024, TILE)))
            return 0
        lax.fori_loop(0, 2 * CHUNKS[k][1] // TILE, step, 0)

    def forward(k):
        def to_core(at):
            def store(cols, value):
                PC[k][at, :, cols] = value.astype(BF16)
            return store

        def to_x(cols, value):
            PX[k][:, cols] = (value + RC[k][1 - xh, :, cols].astype(F32)).astype(BF16)

        def to_own(cols, value):
            PO[k][:, cols] = value

        core = {"c": 1 - c}
        partial(k, 2 * (1 - xh) + 1 - c, to_core(1 - xh))
        far = go(PC[k].at[1 - xh], RC[k].at[1 - xh], ms.at[k, 0], mr.at[k, 0], core)
        partial(k, 2 * xh + 1 - c, to_core(xh))
        near = go(PC[k].at[xh], RC[k].at[xh], ms.at[k, 1], mr.at[k, 1], core)
        far.wait_recv()
        partial(k, 2 * (1 - xh) + c, to_x)
        across = go(PX[k], RX[k], ms.at[k, 2], mr.at[k, 2], {"xh": 1 - xh})
        partial(k, 2 * xh + c, to_own)
        return near, across

    def middle(k):
        at, wide = CHUNKS[k]
        me = 2 * xh + c

        def step(i, _):
            rows = pl.ds(pl.multiple_of(i * 16, 16), 16)
            pre = PO[k][rows, :] + RC[k][xh, rows, :].astype(F32) + RX[k][rows, :].astype(F32)
            gate_pre, up_pre = pre[:, :wide], pre[:, wide:]
            sigma = jax.nn.sigmoid(gate_pre)
            activation = gate_pre * sigma
            upstream = cot[rows, pl.ds(at, wide)].astype(F32)
            slope = sigma * (1.0 + gate_pre * (1.0 - sigma))
            hidden[rows, pl.ds(at, wide)] = (activation * up_pre).astype(BF16)
            G[k][me, rows, pl.ds(0, wide)] = (upstream * up_pre * slope).astype(BF16)
            G[k][me, rows, pl.ds(wide, wide)] = (upstream * activation).astype(BF16)
            return 0

        lax.fori_loop(0, 16, step, 0)
        return (
            go(G[k].at[me], G[k].at[me], ms.at[k, 3], mr.at[k, 3], {"xh": 1 - xh}),
            go(G[k].at[me], G[k].at[me], ms.at[k, 4], mr.at[k, 4], {"c": 1 - c}),
        )

    def pass_on(k):
        at = 2 * (1 - xh) + c
        return go(G[k].at[at], G[k].at[at], ms.at[k, 5], mr.at[k, 5], {"c": 1 - c})

    near0, across0 = forward(0)
    arrived(relay1)
    near1, across1 = forward(1)

    def turn(i, _):
        at, j = i // 4, lax.rem(i, 4)
        cols = columns(j)
        xt[cols, columns(at)] = x[at, :, :, :, cols].reshape(256, TILE).T
        return 0

    lax.fori_loop(0, 16, turn, 0)

    near0.wait_recv()
    across0.wait_recv()
    xg0, cg0 = middle(0)
    near1.wait_recv()
    across1.wait_recv()
    xg1, cg1 = middle(1)
    cg0.wait_recv()
    cg1.wait_recv()

    def back(group):
        def step(i, _):
            at, j = 2 * group + i // 4, lax.rem(i, 4)
            total = dot_nt(G[0][at], W[0][j]) + dot_nt(G[1][at], W[1][j])
            dx[at, :, :, :, columns(j)] = total.reshape(2, NZ, 16, TILE)
            return 0
        lax.fori_loop(0, 8, step, 0)

    def z_sum(h, group, step, came):
        out = []
        for way in range(2):
            to = {"z": zm if way else zp}
            far = STEPS - step
            dest = lax.rem(z + (NZ - far if way else far), NZ)
            if step == 0:
                zs[h, way, 0, 0] = dx[2 * group + way, :, dest].astype(BF16)
                out.append(go(zs.at[h, way, 0, 0], zr.at[h, way, 0, 0], zrs.at[h, 0, way], zrr.at[h, 0, way], to))
                continue
            came[way].wait_recv()
            if step == 1:
                zs[h, way, 1, way] = (dx[2 * group + way, :, dest] + zr[h, way, 0, 0].astype(F32)).astype(BF16)
                zs[h, way, 1, 1 - way] = dx[2 * group + 1 - way, :, dest].astype(BF16)
            else:
                for b in range(2):
                    zs[h, way, step, b] = (dx[2 * group + b, :, dest] + zr[h, way, step - 1, b].astype(F32)).astype(BF16)
            out.append(go(zs.at[h, way, step], zr.at[h, way, step], zrs.at[h, step, way], zrr.at[h, step, way], to))
        return out

    def z_last(h, group, came):
        arrived(came)
        out = []
        for b in range(2):
            total = dx[2 * group + b, :, z] + zr[h, 0, 3, b].astype(F32) + zr[h, 1, 3, b].astype(F32)
            ts[group, b] = total.astype(BF16)
        for k, key in enumerate(CUBE):
            a, b, d = flip(*key)
            if key[0] == h and k:
                out.append(go(ts.at[a, b, d], tr.at[xh, c, xl], fs.at[k - 1], fr.at[k - 1], cube_id(*key)))
        if h == 0:
            keep = pltpu.make_async_copy(ts.at[xh, c, xl], tr.at[xh, c, xl], loc.at[5])
            keep.start()
            keep.wait()
        return out

    back(xh)
    zc = z_sum(0, xh, 0, None)

    def weight_grad(k, at):
        def step(j, _):
            cols = columns(j)
            rows = columns(at)
            DW[k][at, :, cols] = dot(xt[rows, :], G[k][:, :, cols].reshape(1024, TILE)).astype(BF16)
            return 0
        lax.fori_loop(0, 2 * CHUNKS[k][1] // TILE, step, 0)

    upper, lower = pl.ds(0, 128), pl.ds(128, 128)

    def sums_out(k):
        weight_grad(k, y2)
        a = go(DW[k].at[y2, upper], QY[k].at[0], ys.at[k, 0], yr.at[k, 0], {"y": yp})
        b = go(DW[k].at[y2, lower], QY[k].at[1], ys.at[k, 1], yr.at[k, 1], {"y": ym})
        weight_grad(k, yp)
        e = go(DW[k].at[yp, lower], RY[k].at[0, lower], ys.at[k, 2], yr.at[k, 2], {"y": yp})
        weight_grad(k, ym)
        f = go(DW[k].at[ym, upper], RY[k].at[1, upper], ys.at[k, 3], yr.at[k, 3], {"y": ym})
        weight_grad(k, y)
        return a, b, e, f

    def sums_on(k, a, b):
        a.wait_recv()
        DW[k][yp, upper] = (DW[k][yp, upper].astype(F32) + QY[k][0].astype(F32)).astype(BF16)
        e = go(DW[k].at[yp, upper], RY[k].at[0, upper], ys.at[k, 4], yr.at[k, 4], {"y": yp})
        b.wait_recv()
        DW[k][ym, lower] = (DW[k][ym, lower].astype(F32) + QY[k][1].astype(F32)).astype(BF16)
        f = go(DW[k].at[ym, lower], RY[k].at[1, lower], ys.at[k, 5], yr.at[k, 5], {"y": ym})
        return e, f

    def sums_in(k, copies):
        at, wide = CHUNKS[k]
        arrived(copies)

        def step(i, _):
            rows = pl.ds(pl.multiple_of(i * 32, 32), 32)
            total = DW[k][y, rows].astype(F32) + RY[k][0, rows].astype(F32) + RY[k][1, rows].astype(F32)
            total = total.astype(BF16)
            grad_gate[rows, pl.ds(at, wide)] = total[:, :wide]
            grad_up[rows, pl.ds(at, wide)] = total[:, wide:]
            return 0

        lax.fori_loop(0, 8, step, 0)

    xg0.wait_recv()
    pass0 = pass_on(0)
    zc = z_sum(0, xh, 1, zc)
    pass0.wait_recv()
    y0 = sums_out(0)
    zc = z_sum(0, xh, 2, zc)
    xg1.wait_recv()
    pass1 = pass_on(1)
    zc = z_sum(0, xh, 3, zc)
    pass1.wait_recv()
    back(1 - xh)
    zd = z_sum(1, 1 - xh, 0, None)
    y0n = sums_on(0, y0[0], y0[1])
    y1 = sums_out(1)
    zd = z_sum(1, 1 - xh, 1, zd)
    end0 = z_last(0, xh, zc)
    zd = z_sum(1, 1 - xh, 2, zd)
    y1n = sums_on(1, y1[0], y1[1])
    zd = z_sum(1, 1 - xh, 3, zd)
    sums_in(0, (y0[2], y0[3], *y0n))
    end1 = z_last(1, 1 - xh, zd)
    sums_in(1, (y1[2], y1[3], *y1n))
    arrived(end0)
    arrived(end1)
    for a in range(2):
        for b in range(2):
            rows_out[2 * a + b] = (tr[a, b, 0].astype(F32) + tr[a, b, 1].astype(F32)).astype(BF16)
    for copy in sent:
        copy.wait_send()


def body(tokens, gate_weight, up_weight, cotangent):
    rows, model = tokens.shape
    depth, width = gate_weight.shape
    nx, ny, nc = (lax.axis_size(a) for a in DP)
    cut = tokens.reshape(rows, nx, ny, nc, depth).transpose(1, 3, 0, 2, 4)
    cut = cut.reshape(nx * nc, rows, ny * depth)
    wides = [2 * wide for _, wide in CHUNKS]
    dma = pltpu.SemaphoreType.DMA

    def per_chunk(*lead, dtype=BF16):
        return [pltpu.VMEM((*lead, wide), dtype) for wide in wides]

    vmem = pl.BlockSpec(memory_space=pltpu.VMEM)
    grid = pl.BlockSpec(memory_space=pl.ANY)
    tile = jax.ShapeDtypeStruct((depth, width), BF16)
    hidden, back, grad_gate, grad_up = pl.pallas_call(
        kernel,
        out_shape=(tile, jax.ShapeDtypeStruct((nx * nc, rows, ny * depth), BF16), tile, tile),
        in_specs=[vmem, grid, grid, vmem],
        out_specs=(vmem, vmem, vmem, vmem),
        scratch_shapes=[
            pltpu.VMEM((4, 2, NZ, 16, 1024), BF16),
            pltpu.VMEM((1024, 1024), BF16),
            *per_chunk(4, 256),
            *per_chunk(2, 256),
            *per_chunk(2, 256),
            *per_chunk(256),
            *per_chunk(256),
            *per_chunk(256, dtype=F32),
            *per_chunk(4, 256),
            *per_chunk(4, 256),
            *per_chunk(2, 256),
            *per_chunk(2, 128),
            pltpu.VMEM((4, 2, NZ, 16, 1024), F32),
            pltpu.VMEM((2, 2, STEPS, 2, 2, 16, 1024), BF16),
            pltpu.VMEM((2, 2, STEPS, 2, 2, 16, 1024), BF16),
            pltpu.VMEM((2, 2, 2, 16, 1024), BF16),
            pltpu.VMEM((2, 2, 2, 16, 1024), BF16),
            dma((6,)), dma((7,)), dma((7,)),
            dma((4, 2, 2)), dma((4, 2, 2)),
            dma((2, 4)), dma((2, 4)),
            dma((2, 6)), dma((2, 6)),
            dma((2, 6)), dma((2, 6)),
            dma((2, STEPS, 2)), dma((2, STEPS, 2)),
            dma((7,)), dma((7,)),
        ],
        compiler_params=pltpu.CompilerParams(
            collective_id=0, has_side_effects=True, vmem_limit_bytes=56 * 2**20
        ),
        name="swiglu",
    )(cut, gate_weight, up_weight, cotangent)
    back = back.reshape(nx, nc, rows, ny, depth).transpose(2, 0, 3, 1, 4).reshape(rows, model)
    return (hidden, back, grad_gate, grad_up)


def solution(mesh):
    torus = Mesh(mesh.devices.reshape(2, 4, 2, 2, 8), (*DP, *TENSOR))
    specs = (ROWS, BLOCK, BLOCK, BLOCK)
    outs = (BLOCK, ROWS, BLOCK, BLOCK)
    return jax.shard_map(body, mesh=torus, in_specs=specs, out_specs=outs, check_vma=False)
```

time: 427 us -> 130 us (0.30)
  waiting for transfers between devices: 352 us -> 0 us
  Pallas kernels: 0 us -> 122 us
  matrix products: 24.7 us -> 0 us
  between operations: 14.2 us -> 0.67 us
  blocking collectives: 11.4 us -> 0 us
  local copies, waits for them, and re-layouts: 13.7 us -> 6.8 us
  starting transfers between devices: 5.55 us -> 0 us
  other arithmetic: 5.14 us -> 0 us
    all_gather x3 -> x0, waiting for transfers between devices: 154 us -> none  [the longest x1 60.2 us: body(): mine = lax.all_gather(cut, TENSOR, axis=1, tiled=True)]
    pallas_call x0 -> x1, Pallas kernels: none -> 122 us  [body(): pl.pallas_call(kernel, out_shape=(tile, jax.ShapeDtypeStruct((nx * nc, ro...]
    unnamed x9 -> x0, waiting for transfers between devices: 106 us -> none
    reduce_scatter x2 -> x0, waiting for transfers between devices: 88.3 us -> none  [the longest x1 52.5 us: body(): lax.psum_scatter(part, SPLIT, scatter_dimension=0, tiled=True)]
    dot_general x3 -> x0, matrix products: 24.7 us -> none  [the longest x1 8.59 us: body(): jnp.dot(mine, weights, preferred_element_type=jnp.float32)]
    all_to_all x1 -> x0, blocking collectives: 11.4 us -> none  [body(): cut = lax.all_to_all(cut, SPLIT, 0, 0, tiled=True)]
    all_to_all x1 -> x0, starting transfers between devices: 5.08 us -> none  [body(): back = lax.all_to_all(back, SPLIT, 0, 0, tiled=True)]
    squeeze x2 -> x0, local copies, waits for them, and re-layouts: 4.54 us -> none  [the longest x1 2.32 us: body(): back = lax.psum_scatter(back, 'z', scatter_dimension=0, tiled=True)[0]]
  transfers between devices with their start and end apart: 8 -> 0, of which waited for: 8 -> 0; matrix products, arithmetic and copies ran while one was open for 4% -> 0% of each run, Pallas kernels for 0% -> 0%
where the time goes in v2:
time: 130 us; the launch traced here: 129 us
  Pallas kernels  122 us (94%)
  local copies, waits for them, and re-layouts  6.8 us (5%)
    pallas_call x1, Pallas kernels, body(): pl.pallas_call(kernel, out_shape=(tile, jax.ShapeDtypeStruct((nx * nc, ro...  122 us
    unnamed x9, local copies, waits for them, and re-layouts  3.14 us

profile of v2, /device:TPU:1, one launch (start us, length us, event | category | flops | bytes accessed | tf_op | source)
XLA Modules:
  0.0 129.5 jit_solution(11030479739413090727)
XLA Ops:
  0.6 1.0 reshape.20
  1.6 0.1 copy.11
  1.7 0.7 reshape.21.tokens
  2.4 122.0 %swiglu.1 = (bf16[256,896]{1,0:T(8,128)(2,1)}, bf16[4,16,1024]{2,1,0:T(8,128)(2,1)}, bf16[256,896]{1,0:T(8,128)(2,1)}, bf16[256,896]{1,0:T(8,128)(2,1)}) custom-call(bf16[4,16,1024]{2,1,0:T(8,128)(2,1)} %reshape.21.tokens, bf16[256,896]{1,0:T(8,128)(2,1)} %gate.1, bf16[256,896]{1,0:T(8,128)(2,1)} %up.1, bf16[256,896]{1,0:T(8,128)(2,1)} %cot.1), custom_call_target="tpu_custom_call" | custom-call | tf_op jit(solution)/shard_map/swiglu/pallas_call | solution.py:360
  124.4 0.0 copy-start.2
  124.4 1.0 reshape.22
  125.5 0.1 copy.9
  125.6 0.7 reshape.23
  126.3 0.0 copy-done.2
  126.4 0.0 copy-start.1
  126.4 0.8 copy.15
  127.1 0.4 copy-done.1
  127.5 0.0 copy-start
  127.5 0.8 copy.16
  128.3 0.4 copy-done
  128.7 0.8 copy.17
Async XLA Ops:
  124.4 1.9 %copy-start.2 = (bf16[256,896]{1,0:T(8,128)(2,1)S(1)}, bf16[256,896]{1,0:T(8,128)(2,1)}, u32[]{:S(2)}) copy-start(bf16[256,896]{1,0:T(8,128)(2,1)} %get-tuple-element.16) | copy-start | bytes 1376260
  126.4 1.2 copy-start.1
  127.5 1.2 copy-start

commit v3 on v1

v3 whole, which is shorter than its diff:
```python
import functools

import jax
import jax.numpy as jnp
from jax import lax
from jax.experimental import pallas as pl
from jax.experimental.pallas import tpu as pltpu
from jax.sharding import Mesh
from jax.sharding import PartitionSpec as P

SPLIT = ("xh", "c")
TENSOR = ("xl", "z")
DP = ("xh", "y", "c")
ROWS = P((*DP, *TENSOR), None)
BLOCK = P(DP, TENSOR)
MESH = pl.DeviceIdType.MESH
F32 = jnp.float32
BF16 = jnp.bfloat16
CHUNKS = ((0, 256), (256, 384), (640, 256))
NZ = 8
TILE = 256
OFFSETS = (0, 1, -1, 2, -2, 3, -3, 4)
CUBE = tuple((a, b, d) for a in range(2) for b in range(2) for d in range(2))
STEPS = 4


def dot(a, b):
    return jnp.dot(a, b, preferred_element_type=F32)


def dot_nt(a, b):
    return lax.dot_general(a, b, (((1,), (1,)), ((), ())), preferred_element_type=F32)


def kernel(tokens, gate, up, cot, hidden, rows_out, grad_gate, grad_up, *scratch):
    n = len(CHUNKS)
    W, PC, RC, PX, RX, PO, G, DW, RY, QY = (scratch[i * n : (i + 1) * n] for i in range(10))
    (
        x, xt, stage, dx, zs, zr, ts, tr,
        loc, cs, cr, zgs, zgr, ws, wr, ms, mr, ys, yr, zrs, zrr, fs, fr,
    ) = scratch[10 * n :]
    xh, y, c, xl, z = (lax.axis_index(a) for a in ("xh", "y", "c", "xl", "z"))
    yp, ym, y2 = lax.rem(y + 1, 4), lax.rem(y + 3, 4), lax.rem(y + 2, 4)
    zp, zm = lax.rem(z + 1, NZ), lax.rem(z + NZ - 1, NZ)
    core, across = {"c": 1 - c}, {"xh": 1 - xh}
    sent = []

    def go(src, dst, send, recv, to):
        copy = pltpu.make_async_remote_copy(
            src_ref=src, dst_ref=dst, send_sem=send, recv_sem=recv,
            device_id=to, device_id_type=MESH,
        )
        copy.start()
        sent.append(copy)
        return copy

    def arrived(copies):
        for copy in copies:
            copy.wait_recv()

    def flip(a, b, d):
        return (1 - xh if a else xh, 1 - c if b else c, 1 - xl if d else xl)

    def cube_id(a, b, d):
        px, pc, plo = flip(a, b, d)
        return {"xh": px, "c": pc, "xl": plo}

    def slot(offset):
        return divmod(OFFSETS.index(offset if offset != -4 else 4), 4)

    def half(hs):
        return pl.ds(hs[0], len(hs))

    local = []
    for k, (at, wide) in enumerate(CHUNKS):
        for i, ref in enumerate((gate, up)):
            copy = pltpu.make_async_copy(
                ref.at[:, pl.ds(at, wide)], W[k].at[y, :, pl.ds(i * wide, wide)], loc.at[2 * k + i]
            )
            copy.start()
            local.append(copy)
    for a in range(2):
        for b in range(2):
            for i in range(4):
                at = ((a * 4 + i) * 2 + b) * 256
                stage[2 * a + b, :, i * 256 : (i + 1) * 256] = tokens[:, at : at + 256]
    x[0, c, xh, xl, 0] = stage[2 * xh + c]

    barrier = pltpu.get_barrier_semaphore()
    peers = [{"y": yp}, {"y": ym}, {"z": zp}, {"z": zm}] + [cube_id(*k) for k in CUBE[1:]]
    for peer in peers:
        pl.semaphore_signal(barrier, inc=1, device_id=peer, device_id_type=MESH)
    pl.semaphore_wait(barrier, len(peers))

    cube = [None]
    for k, key in enumerate(CUBE):
        if k:
            a, b, _ = flip(*key)
            cube.append(go(stage.at[2 * a + b], x.at[0, c, xh, xl, 0], cs.at[k - 1], cr.at[k - 1], cube_id(*key)))

    def send_weights(k):
        return (
            go(W[k].at[y], W[k].at[y], ws.at[k, 0], wr.at[k, 0], {"y": yp}),
            go(W[k].at[y], W[k].at[y], ws.at[k, 1], wr.at[k, 1], {"y": ym}),
        )

    def relay_weights(k):
        return (
            go(W[k].at[ym, pl.ds(0, 128)], W[k].at[ym, pl.ds(0, 128)], ws.at[k, 2], wr.at[k, 2], {"y": yp}),
            go(W[k].at[yp, pl.ds(128, 128)], W[k].at[yp, pl.ds(128, 128)], ws.at[k, 3], wr.at[k, 3], {"y": ym}),
        )

    for copy in local:
        copy.wait()
    direct = [send_weights(0), send_weights(1)]
    relay = []

    moving = {}

    def z_step(step):
        for i in range(4):
            if step == 0:
                arrived(cube[max(1, 2 * i) : 2 * i + 2])
            px, pc, _ = flip(i // 2, i % 2, 0)
            for way in range(2):
                if (step - 1, i, way) in moving:
                    moving[step - 1, i, way].wait_recv()
                if step == 3 and i // 2 != way:
                    continue
                sign = 1 if way else -1
                (h, at), (h2, to) = slot(sign * step), slot(sign * (step + 1))
                moving[step, i, way] = go(
                    x.at[h, pc, px, :, at], x.at[h2, pc, px, :, to],
                    zgs.at[step, i, way], zgr.at[step, i, way], {"z": zm if way else zp},
                )

    def columns(j):
        return pl.ds(pl.multiple_of(j * TILE, TILE), TILE)

    def matrix(ref, k):
        return ref[k][...].reshape(1024, 2 * CHUNKS[k][1])

    def forward(k, hs):
        sl, m, w = half(hs), len(hs), 2 * CHUNKS[k][1]
        value = dot(x[sl, 1 - c].reshape(256 * m, 1024), matrix(W, k))
        PC[k][sl] = value.astype(BF16).reshape(m, 2, 128, w)
        near = go(PC[k].at[sl], RC[k].at[sl], ms.at[k, hs[0]], mr.at[k, hs[0]], core)
        value = dot(x[sl, c].reshape(256 * m, 1024), matrix(W, k))
        PO[k][sl] = value.reshape(m, 2, 128, w)
        near.wait_recv()
        PX[k][sl] = (PO[k][sl, 1 - xh] + RC[k][sl, 1 - xh].astype(F32)).astype(BF16)

    def sums_across(k, hs):
        sl, i = half(hs), 2 + hs[0]
        return go(PX[k].at[sl], RX[k].at[sl], ms.at[k, i], mr.at[k, i], across)

    def grads_across(k, hs):
        part, i = G[k].at[half(hs), c, xh], 4 + hs[0]
        return go(part, part, ms.at[k, i], mr.at[k, i], across)

    def pass_on(k, hs):
        part, i = G[k].at[half(hs), c, 1 - xh], 7 + hs[0]
        return go(part, part, ms.at[k, i], mr.at[k, i], core)

    def middle(k):
        at, wide = CHUNKS[k]

        def step(i, _):
            h, j = i // 8, lax.rem(i, 8)
            rows = pl.ds(pl.multiple_of(j * 16, 16), 16)
            r = 4 * h + lax.rem(j, 4)
            there = lax.rem(z + NZ + (r + 1) // 2 * (2 * lax.rem(r, 2) - 1), NZ)
            place = pl.ds(pl.multiple_of((j // 4 * NZ + there) * 16, 16), 16)
            pre = PO[k][h, xh, rows, :] + RC[k][h, xh, rows, :].astype(F32) + RX[k][h, rows, :].astype(F32)
            gate_pre, up_pre = pre[:, :wide], pre[:, wide:]
            sigma = jax.nn.sigmoid(gate_pre)
            activation = gate_pre * sigma
            upstream = cot[place, pl.ds(at, wide)].astype(F32)
            slope = sigma * (1.0 + gate_pre * (1.0 - sigma))
            hidden[place, pl.ds(at, wide)] = (activation * up_pre).astype(BF16)
            G[k][h, c, xh, rows, pl.ds(0, wide)] = (upstream * up_pre * slope).astype(BF16)
            G[k][h, c, xh, rows, pl.ds(wide, wide)] = (upstream * activation).astype(BF16)
            return 0

        lax.fori_loop(0, 16, step, 0)
        part = G[k].at[:, c, xh]
        return go(part, part, ms.at[k, 6], mr.at[k, 6], core)

    def turn(i, _):
        at, j = i // 4, lax.rem(i, 4)
        cols = columns(j)
        xt[cols, columns(at)] = x[at // 2, lax.rem(at, 2), :, :, :, :, cols].reshape(256, TILE).T
        return 0

    def back(g, h, chunks, add):
        total = sum(
            dot_nt(G[k][h, :, g].reshape(256, 2 * CHUNKS[k][1]), matrix(W, k)) for k in chunks
        )
        total = total.reshape(2, 2, 4, 16, 1024)
        dx[h, :, g] = total + dx[h, :, g] if add else total

    flows = {}

    def z_sum(h, step):
        for b in range(2):
            gx, gc, _ = flip(h, b, 0)
            for way in range(2):
                if step == 0 and b != way:
                    continue
                far = STEPS - step
                side, at = slot(-far if way else far)
                value = dx[side, gc, gx, :, at]
                if (h, step - 1, way, b) in flows:
                    flows[h, step - 1, way, b].wait_recv()
                    value = value + zr[h, way, step - 1, b].astype(F32)
                zs[h, way, step, b] = value.astype(BF16)
                flows[h, step, way, b] = go(
                    zs.at[h, way, step, b], zr.at[h, way, step, b],
                    zrs.at[h, step, way, b], zrr.at[h, step, way, b], {"z": zm if way else zp},
                )

    def z_last(h):
        out = []
        for b in range(2):
            arrived((flows[h, 3, 0, b], flows[h, 3, 1, b]))
            gx, gc, _ = flip(h, b, 0)
            total = dx[0, gc, gx, :, 0] + zr[h, 0, 3, b].astype(F32) + zr[h, 1, 3, b].astype(F32)
            ts[gx, gc] = total.astype(BF16)
            for d in range(2):
                key = (h, b, d)
                k = CUBE.index(key)
                at = flip(*key)
                if k:
                    out.append(go(ts.at[at], tr.at[xh, c, xl], fs.at[k - 1], fr.at[k - 1], cube_id(*key)))
        if h == 0:
            tr[xh, c, xl] = ts[xh, c, xl]
        return out

    def weight_grad(k, at):
        DW[k][at] = dot(xt[columns(at), :], matrix(G, k)).astype(BF16)

    upper, lower = pl.ds(0, 128), pl.ds(128, 128)

    def sums_out(k):
        weight_grad(k, y2)
        a = go(DW[k].at[y2, upper], QY[k].at[0], ys.at[k, 0], yr.at[k, 0], {"y": yp})
        b = go(DW[k].at[y2, lower], QY[k].at[1], ys.at[k, 1], yr.at[k, 1], {"y": ym})
        weight_grad(k, yp)
        e = go(DW[k].at[yp, lower], RY[k].at[0, lower], ys.at[k, 2], yr.at[k, 2], {"y": yp})
        weight_grad(k, ym)
        f = go(DW[k].at[ym, upper], RY[k].at[1, upper], ys.at[k, 3], yr.at[k, 3], {"y": ym})
        weight_grad(k, y)
        return a, b, e, f

    def sums_on(k, a, b):
        a.wait_recv()
        DW[k][yp, upper] = (DW[k][yp, upper].astype(F32) + QY[k][0].astype(F32)).astype(BF16)
        e = go(DW[k].at[yp, upper], RY[k].at[0, upper], ys.at[k, 4], yr.at[k, 4], {"y": yp})
        b.wait_recv()
        DW[k][ym, lower] = (DW[k][ym, lower].astype(F32) + QY[k][1].astype(F32)).astype(BF16)
        f = go(DW[k].at[ym, lower], RY[k].at[1, lower], ys.at[k, 5], yr.at[k, 5], {"y": ym})
        return e, f

    def sums_in(k, copies):
        at, wide = CHUNKS[k]
        arrived(copies)

        def step(i, _):
            rows = pl.ds(pl.multiple_of(i * 32, 32), 32)
            total = DW[k][y, rows].astype(F32) + RY[k][0, rows].astype(F32) + RY[k][1, rows].astype(F32)
            total = total.astype(BF16)
            grad_gate[rows, pl.ds(at, wide)] = total[:, :wide]
            grad_up[rows, pl.ds(at, wide)] = total[:, wide:]
            return 0

        lax.fori_loop(0, 8, step, 0)

    z_step(0)
    z_step(1)
    arrived(direct[0])
    relay.append(relay_weights(0))
    z_step(2)
    arrived(relay[0])
    forward(0, (0,))
    a0 = sums_across(0, (0,))
    arrived(direct[1])
    relay.append(relay_weights(1))
    direct.append(send_weights(2))
    z_step(3)
    arrived([moving[key] for key in moving if key[0] == 3])
    forward(0, (1,))
    a0.wait_send()
    b0 = sums_across(0, (1,))
    lax.fori_loop(0, 8, turn, 0)
    arrived(relay[1])
    forward(1, (0, 1))
    b0.wait_send()
    s1 = sums_across(1, (0, 1))
    a0.wait_recv()
    b0.wait_recv()
    c0 = middle(0)
    arrived(direct[2])
    relay.append(relay_weights(2))
    lax.fori_loop(8, 16, turn, 0)
    arrived(relay[2])
    forward(2, (0, 1))
    s1.wait_send()
    g0 = grads_across(0, (0, 1))
    s1.wait_recv()
    c1 = middle(1)
    g0.wait_send()
    s2 = sums_across(2, (0, 1))
    g0.wait_recv()
    p0 = pass_on(0, (0, 1))
    arrived((c0, p0))
    y0 = sums_out(0)
    s2.wait_send()
    g1 = grads_across(1, (0, 1))
    s2.wait_recv()
    c2 = middle(2)
    arrived((c1, c2))
    back(xh, 1, (0, 1, 2), False)
    z_sum(0, 0)
    back(xh, 0, (0, 1, 2), False)
    y0n = sums_on(0, y0[0], y0[1])
    g1.wait_send()
    g2b = grads_across(2, (1,))
    z_sum(0, 1)
    g2b.wait_send()
    g2a = grads_across(2, (0,))
    g1.wait_recv()
    p1 = pass_on(1, (0, 1))
    z_sum(0, 2)
    p1.wait_recv()
    back(1 - xh, 1, (0, 1), False)
    g2b.wait_recv()
    p2b = pass_on(2, (1,))
    back(1 - xh, 0, (0, 1), False)
    p2b.wait_recv()
    back(1 - xh, 1, (2,), True)
    z_sum(1, 0)
    g2a.wait_recv()
    p2a = pass_on(2, (0,))
    y1 = sums_out(1)
    z_sum(1, 1)
    p2a.wait_recv()
    back(1 - xh, 0, (2,), True)
    z_sum(0, 3)
    y1n = sums_on(1, y1[0], y1[1])
    y2s = sums_out(2)
    z_sum(1, 2)
    end0 = z_last(0)
    y2n = sums_on(2, y2s[0], y2s[1])
    sums_in(0, (y0[2], y0[3], *y0n))
    z_sum(1, 3)
    sums_in(1, (y1[2], y1[3], *y1n))
    end1 = z_last(1)
    sums_in(2, (y2s[2], y2s[3], *y2n))
    arrived(end0)
    arrived(end1)
    for a in range(2):
        for b in range(2):
            total = (tr[a, b, 0].astype(F32) + tr[a, b, 1].astype(F32)).astype(BF16)
            for i in range(4):
                at = ((a * 4 + i) * 2 + b) * 256
                rows_out[:, at : at + 256] = total[:, i * 256 : (i + 1) * 256]
    gated = (a0, b0, s1, s2, g0, g1, g2b)
    for copy in sent:
        if not any(copy is one for one in gated):
            copy.wait_send()


def body(tokens, gate_weight, up_weight, cotangent):
    wides = [2 * wide for _, wide in CHUNKS]
    n = len(CHUNKS)
    dma = pltpu.SemaphoreType.DMA

    def per_chunk(*lead, dtype=BF16):
        return [pltpu.VMEM((*lead, wide), dtype) for wide in wides]

    vmem = pl.BlockSpec(memory_space=pltpu.VMEM)
    grid = pl.BlockSpec(memory_space=pl.ANY)
    tile = jax.ShapeDtypeStruct(gate_weight.shape, BF16)
    return pl.pallas_call(
        kernel,
        out_shape=(tile, jax.ShapeDtypeStruct(tokens.shape, BF16), tile, tile),
        in_specs=[vmem, grid, grid, vmem],
        out_specs=(vmem, vmem, vmem, vmem),
        scratch_shapes=[
            *per_chunk(4, 256),
            *per_chunk(2, 2, 128),
            *per_chunk(2, 2, 128),
            *per_chunk(2, 128),
            *per_chunk(2, 128),
            *per_chunk(2, 2, 128, dtype=F32),
            *per_chunk(2, 2, 2, 128),
            *per_chunk(4, 256),
            *per_chunk(2, 256),
            *per_chunk(2, 128),
            pltpu.VMEM((2, 2, 2, 2, 4, 16, 1024), BF16),
            pltpu.VMEM((1024, 1024), BF16),
            pltpu.VMEM((4, 16, 1024), BF16),
            pltpu.VMEM((2, 2, 2, 2, 4, 16, 1024), F32),
            pltpu.VMEM((2, 2, STEPS, 2, 2, 16, 1024), BF16),
            pltpu.VMEM((2, 2, STEPS, 2, 2, 16, 1024), BF16),
            pltpu.VMEM((2, 2, 2, 16, 1024), BF16),
            pltpu.VMEM((2, 2, 2, 16, 1024), BF16),
            dma((2 * n,)), dma((7,)), dma((7,)),
            dma((4, 4, 2)), dma((4, 4, 2)),
            dma((n, 4)), dma((n, 4)),
            dma((n, 9)), dma((n, 9)),
            dma((n, 6)), dma((n, 6)),
            dma((2, STEPS, 2, 2)), dma((2, STEPS, 2, 2)),
            dma((7,)), dma((7,)),
        ],
        compiler_params=pltpu.CompilerParams(
            collective_id=0, has_side_effects=True, vmem_limit_bytes=56 * 2**20
        ),
        name="swiglu",
    )(tokens, gate_weight, up_weight, cotangent)


def solution(mesh):
    torus = Mesh(mesh.devices.reshape(2, 4, 2, 2, 8), (*DP, *TENSOR))
    specs = (ROWS, BLOCK, BLOCK, BLOCK)
    outs = (BLOCK, ROWS, BLOCK, BLOCK)
    return jax.shard_map(body, mesh=torus, in_specs=specs, out_specs=outs, check_vma=False)
```

time: 427 us -> 119 us (0.28)
  waiting for transfers between devices: 352 us -> 0 us
  Pallas kernels: 0 us -> 114 us
  matrix products: 24.7 us -> 0 us
  between operations: 14.2 us -> 0.66 us
  blocking collectives: 11.4 us -> 0 us
  local copies, waits for them, and re-layouts: 13.7 us -> 4.5 us
  starting transfers between devices: 5.55 us -> 0 us
  other arithmetic: 5.14 us -> 0 us
    all_gather x3 -> x0, waiting for transfers between devices: 154 us -> none  [the longest x1 60.2 us: body(): mine = lax.all_gather(cut, TENSOR, axis=1, tiled=True)]
    pallas_call x0 -> x1, Pallas kernels: none -> 114 us  [body(): pl.pallas_call(kernel, out_shape=(tile, jax.ShapeDtypeStruct(tokens.shape...]
    unnamed x9 -> x0, waiting for transfers between devices: 106 us -> none
    reduce_scatter x2 -> x0, waiting for transfers between devices: 88.3 us -> none  [the longest x1 52.5 us: body(): lax.psum_scatter(part, SPLIT, scatter_dimension=0, tiled=True)]
    dot_general x3 -> x0, matrix products: 24.7 us -> none  [the longest x1 8.59 us: body(): jnp.dot(mine, weights, preferred_element_type=jnp.float32)]
    all_to_all x1 -> x0, blocking collectives: 11.4 us -> none  [body(): cut = lax.all_to_all(cut, SPLIT, 0, 0, tiled=True)]
    all_to_all x1 -> x0, starting transfers between devices: 5.08 us -> none  [body(): back = lax.all_to_all(back, SPLIT, 0, 0, tiled=True)]
    squeeze x2 -> x0, local copies, waits for them, and re-layouts: 4.54 us -> none  [the longest x1 2.32 us: body(): back = lax.psum_scatter(back, 'z', scatter_dimension=0, tiled=True)[0]]
  transfers between devices with their start and end apart: 8 -> 0, of which waited for: 8 -> 0; matrix products, arithmetic and copies ran while one was open for 4% -> 0% of each run, Pallas kernels for 0% -> 0%
where the time goes in v3:
time: 119 us
  Pallas kernels  114 us (96%)
  local copies, waits for them, and re-layouts  4.5 us (4%)
    pallas_call x1, Pallas kernels, body(): pl.pallas_call(kernel, out_shape=(tile, jax.ShapeDtypeStruct(tokens.shape...  114 us
    unnamed x10, local copies, waits for them, and re-layouts  4.5 us

profile of v3, /device:TPU:1, one launch (start us, length us, event | category | flops | bytes accessed | tf_op | source)
XLA Modules:
  0.0 119.2 jit_solution(5649999337408653737)
XLA Ops:
  0.6 114.0 %swiglu.1 = (bf16[256,896]{1,0:T(8,128)(2,1)}, bf16[16,4096]{1,0:T(8,128)(2,1)}, bf16[256,896]{1,0:T(8,128)(2,1)}, bf16[256,896]{1,0:T(8,128)(2,1)}) custom-call(bf16[16,4096]{1,0:T(8,128)(2,1)} %tokens.1, bf16[256,896]{1,0:T(8,128)(2,1)} %gate.1, bf16[256,896]{1,0:T(8,128)(2,1)} %up.1, bf16[256,896]{1,0:T(8,128)(2,1)} %cot.1), custom_call_target="tpu_custom_call" | custom-call | tf_op jit(solution)/shard_map/swiglu/pallas_call | solution.py:384
  114.6 0.0 copy-start.2
  114.7 0.0 copy-start.1
  114.7 1.9 %copy.12 = bf16[256,896]{1,0:T(8,128)(2,1)} copy(bf16[256,896]{1,0:T(8,128)(2,1)} %get-tuple-element.8) | data formatting | bytes 917504
  116.5 0.0 copy-done.2
  116.6 0.7 copy.13
  117.2 0.0 copy-done.1
  117.2 0.0 copy-start
  117.2 0.8 copy.14
  118.0 0.4 copy-done
  118.4 0.8 copy.15
Async XLA Ops:
  114.6 1.9 %copy-start.2 = (bf16[16,4096]{1,0:T(8,128)(2,1)S(1)}, bf16[16,4096]{1,0:T(8,128)(2,1)}, u32[]{:S(2)}) copy-start(bf16[16,4096]{1,0:T(8,128)(2,1)} %get-tuple-element.9) | copy-start | bytes 393220
  114.7 2.6 %copy-start.1 = (bf16[256,896]{1,0:T(8,128)(2,1)S(1)}, bf16[256,896]{1,0:T(8,128)(2,1)}, u32[]{:S(2)}) copy-start(bf16[256,896]{1,0:T(8,128)(2,1)} %get-tuple-element.10) | copy-start | bytes 1376260
  117.2 1.2 copy-start

commit v4 on v3

--- a/solution.py
+++ b/solution.py
@@ -32,11 +32,11 @@
     return lax.dot_general(a, b, (((1,), (1,)), ((), ())), preferred_element_type=F32)
 
 
-def kernel(tokens, gate, up, cot, hidden, rows_out, grad_gate, grad_up, *scratch):
+def kernel(tokens, gate, up, cot_far, hidden, rows_out, grad_gate, grad_up, *scratch):
     n = len(CHUNKS)
     W, PC, RC, PX, RX, PO, G, DW, RY, QY = (scratch[i * n : (i + 1) * n] for i in range(10))
     (
-        x, xt, stage, dx, zs, zr, ts, tr,
+        x, xt, stage, cot_here, dx, zs, zr, ts, tr,
         loc, cs, cr, zgs, zgr, ws, wr, ms, mr, ys, yr, zrs, zrr, fs, fr,
     ) = scratch[10 * n :]
     xh, y, c, xl, z = (lax.axis_index(a) for a in ("xh", "y", "c", "xl", "z"))
@@ -54,6 +54,10 @@
         sent.append(copy)
         return copy
 
+    def left(copy):
+        copy.wait_send()
+        sent[:] = [one for one in sent if one is not copy]
+
     def arrived(copies):
         for copy in copies:
             copy.wait_recv()
@@ -71,6 +75,12 @@
     def half(hs):
         return pl.ds(hs[0], len(hs))
 
+    barrier = pltpu.get_barrier_semaphore()
+    peers = [{"y": yp}, {"y": ym}, {"z": zp}, {"z": zm}] + [cube_id(*k) for k in CUBE[1:]]
+    for peer in peers:
+        pl.semaphore_signal(barrier, inc=1, device_id=peer, device_id_type=MESH)
+    cot = cot_here
+    cot_in = pltpu.make_async_copy(cot_far, cot, loc.at[2 * n])
     local = []
     for k, (at, wide) in enumerate(CHUNKS):
         for i, ref in enumerate((gate, up)):
@@ -86,10 +96,6 @@
                 stage[2 * a + b, :, i * 256 : (i + 1) * 256] = tokens[:, at : at + 256]
     x[0, c, xh, xl, 0] = stage[2 * xh + c]
 
-    barrier = pltpu.get_barrier_semaphore()
-    peers = [{"y": yp}, {"y": ym}, {"z": zp}, {"z": zm}] + [cube_id(*k) for k in CUBE[1:]]
-    for peer in peers:
-        pl.semaphore_signal(barrier, inc=1, device_id=peer, device_id_type=MESH)
     pl.semaphore_wait(barrier, len(peers))
 
     cube = [None]
@@ -112,7 +118,8 @@
 
     for copy in local:
         copy.wait()
-    direct = [send_weights(0), send_weights(1)]
+    cot_in.start()
+    direct = [send_weights(0)]
     relay = []
 
     moving = {}
@@ -147,6 +154,10 @@
         near = go(PC[k].at[sl], RC[k].at[sl], ms.at[k, hs[0]], mr.at[k, hs[0]], core)
         value = dot(x[sl, c].reshape(256 * m, 1024), matrix(W, k))
         PO[k][sl] = value.reshape(m, 2, 128, w)
+        return near
+
+    def join(k, hs, near):
+        sl = half(hs)
         near.wait_recv()
         PX[k][sl] = (PO[k][sl, 1 - xh] + RC[k][sl, 1 - xh].astype(F32)).astype(BF16)
 
@@ -249,7 +260,6 @@
         e = go(DW[k].at[yp, lower], RY[k].at[0, lower], ys.at[k, 2], yr.at[k, 2], {"y": yp})
         weight_grad(k, ym)
         f = go(DW[k].at[ym, upper], RY[k].at[1, upper], ys.at[k, 3], yr.at[k, 3], {"y": ym})
-        weight_grad(k, y)
         return a, b, e, f
 
     def sums_on(k, a, b):
@@ -263,6 +273,7 @@
 
     def sums_in(k, copies):
         at, wide = CHUNKS[k]
+        weight_grad(k, y)
         arrived(copies)
 
         def step(i, _):
@@ -276,86 +287,102 @@
         lax.fori_loop(0, 8, step, 0)
 
     z_step(0)
-    z_step(1)
+    for copy in direct[0]:
+        left(copy)
+    direct.append(send_weights(1))
     arrived(direct[0])
     relay.append(relay_weights(0))
+    z_step(1)
     z_step(2)
     arrived(relay[0])
-    forward(0, (0,))
-    a0 = sums_across(0, (0,))
+    near = forward(0, (0,))
     arrived(direct[1])
     relay.append(relay_weights(1))
-    direct.append(send_weights(2))
+    join(0, (0,), near)
+    a0 = sums_across(0, (0,))
     z_step(3)
+    for copy in relay[1]:
+        left(copy)
+    direct += [send_weights(k) for k in range(2, n)]
     arrived([moving[key] for key in moving if key[0] == 3])
-    forward(0, (1,))
-    a0.wait_send()
+    near = forward(0, (1,))
+    arrived(relay[1])
+    join(0, (1,), near)
+    left(a0)
     b0 = sums_across(0, (1,))
-    lax.fori_loop(0, 8, turn, 0)
-    arrived(relay[1])
-    forward(1, (0, 1))
-    b0.wait_send()
-    s1 = sums_across(1, (0, 1))
-    a0.wait_recv()
-    b0.wait_recv()
-    c0 = middle(0)
-    arrived(direct[2])
-    relay.append(relay_weights(2))
-    lax.fori_loop(8, 16, turn, 0)
-    arrived(relay[2])
-    forward(2, (0, 1))
-    s1.wait_send()
-    g0 = grads_across(0, (0, 1))
-    s1.wait_recv()
-    c1 = middle(1)
-    g0.wait_send()
-    s2 = sums_across(2, (0, 1))
-    g0.wait_recv()
-    p0 = pass_on(0, (0, 1))
-    arrived((c0, p0))
-    y0 = sums_out(0)
-    s2.wait_send()
-    g1 = grads_across(1, (0, 1))
-    s2.wait_recv()
-    c2 = middle(2)
-    arrived((c1, c2))
-    back(xh, 1, (0, 1, 2), False)
+    near = forward(1, (0, 1))
+    lax.fori_loop(0, 16, turn, 0)
+    join(1, (0, 1), near)
+    left(b0)
+    sums = [None, sums_across(1, (0, 1))]
+    arrived((a0, b0))
+    cot_in.wait()
+    own = [middle(0)]
+    for k in range(2, n):
+        arrived(direct[k])
+        relay.append(relay_weights(k))
+    grads, passed, out, on = [], [], [], []
+    for k in range(n - 2):
+        left(sums[k + 1])
+        grads.append(grads_across(k, (0, 1)))
+        arrived(relay[k + 2])
+        near = forward(k + 2, (0, 1))
+        sums[k + 1].wait_recv()
+        own.append(middle(k + 1))
+        join(k + 2, (0, 1), near)
+        left(grads[k])
+        sums.append(sums_across(k + 2, (0, 1)))
+        grads[k].wait_recv()
+        passed.append(pass_on(k, (0, 1)))
+        if k:
+            on.append(sums_on(k - 1, *out[k - 1][:2]))
+        arrived((own[k], passed[k]))
+        out.append(sums_out(k))
+    p, l = n - 2, n - 1
+    most, every = tuple(range(n - 1)), tuple(range(n))
+    left(sums[l])
+    grads.append(grads_across(p, (0, 1)))
+    sums[l].wait_recv()
+    own.append(middle(l))
+    on.append(sums_on(p - 1, *out[p - 1][:2]))
+    arrived((own[p], own[l]))
+    back(xh, 1, every, False)
     z_sum(0, 0)
-    back(xh, 0, (0, 1, 2), False)
-    y0n = sums_on(0, y0[0], y0[1])
-    g1.wait_send()
-    g2b = grads_across(2, (1,))
+    back(xh, 0, every, False)
+    left(grads[p])
+    far = grads_across(l, (1,))
+    grads[p].wait_recv()
+    passed.append(pass_on(p, (0, 1)))
     z_sum(0, 1)
-    g2b.wait_send()
-    g2a = grads_across(2, (0,))
-    g1.wait_recv()
-    p1 = pass_on(1, (0, 1))
+    left(far)
+    near = grads_across(l, (0,))
+    passed[p].wait_recv()
+    out.append(sums_out(p))
+    far.wait_recv()
+    far = pass_on(l, (1,))
+    back(1 - xh, 1, most, False)
+    far.wait_recv()
+    back(1 - xh, 1, (l,), True)
+    z_sum(1, 0)
+    near.wait_recv()
+    near = pass_on(l, (0,))
+    back(1 - xh, 0, most, False)
     z_sum(0, 2)
-    p1.wait_recv()
-    back(1 - xh, 1, (0, 1), False)
-    g2b.wait_recv()
-    p2b = pass_on(2, (1,))
-    back(1 - xh, 0, (0, 1), False)
-    p2b.wait_recv()
-    back(1 - xh, 1, (2,), True)
-    z_sum(1, 0)
-    g2a.wait_recv()
-    p2a = pass_on(2, (0,))
-    y1 = sums_out(1)
+    on.append(sums_on(p, *out[p][:2]))
     z_sum(1, 1)
-    p2a.wait_recv()
-    back(1 - xh, 0, (2,), True)
+    near.wait_recv()
+    back(1 - xh, 0, (l,), True)
+    out.append(sums_out(l))
+    z_sum(1, 2)
     z_sum(0, 3)
-    y1n = sums_on(1, y1[0], y1[1])
-    y2s = sums_out(2)
-    z_sum(1, 2)
+    for k in range(p):
+        sums_in(k, (*out[k][2:], *on[k]))
+    z_sum(1, 3)
+    on.append(sums_on(l, *out[l][:2]))
     end0 = z_last(0)
-    y2n = sums_on(2, y2s[0], y2s[1])
-    sums_in(0, (y0[2], y0[3], *y0n))
-    z_sum(1, 3)
-    sums_in(1, (y1[2], y1[3], *y1n))
+    sums_in(p, (*out[p][2:], *on[p]))
     end1 = z_last(1)
-    sums_in(2, (y2s[2], y2s[3], *y2n))
+    sums_in(l, (*out[l][2:], *on[l]))
     arrived(end0)
     arrived(end1)
     for a in range(2):
@@ -364,10 +391,22 @@
             for i in range(4):
                 at = ((a * 4 + i) * 2 + b) * 256
                 rows_out[:, at : at + 256] = total[:, i * 256 : (i + 1) * 256]
-    gated = (a0, b0, s1, s2, g0, g1, g2b)
     for copy in sent:
-        if not any(copy is one for one in gated):
-            copy.wait_send()
+        copy.wait_send()
+
+
+def hand_over(*refs):
+    n = len(refs) // 3
+    here = refs[2 * n : 3 * n]
+    into = [pltpu.make_async_copy(refs[i], here[i], refs[-1].at[i]) for i in range(n)]
+    out = [pltpu.make_async_copy(here[i], refs[n + i], refs[-1].at[n + i]) for i in range(n)]
+    for copy in into:
+        copy.start()
+    for i in range(n):
+        into[i].wait()
+        out[i].start()
+    for copy in out:
+        copy.wait()
 
 
 def body(tokens, gate_weight, up_weight, cotangent):
@@ -381,10 +420,10 @@
     vmem = pl.BlockSpec(memory_space=pltpu.VMEM)
     grid = pl.BlockSpec(memory_space=pl.ANY)
     tile = jax.ShapeDtypeStruct(gate_weight.shape, BF16)
-    return pl.pallas_call(
+    outs = pl.pallas_call(
         kernel,
         out_shape=(tile, jax.ShapeDtypeStruct(tokens.shape, BF16), tile, tile),
-        in_specs=[vmem, grid, grid, vmem],
+        in_specs=[vmem, grid, grid, grid],
         out_specs=(vmem, vmem, vmem, vmem),
         scratch_shapes=[
             *per_chunk(4, 256),
@@ -400,12 +439,13 @@
             pltpu.VMEM((2, 2, 2, 2, 4, 16, 1024), BF16),
             pltpu.VMEM((1024, 1024), BF16),
             pltpu.VMEM((4, 16, 1024), BF16),
+            pltpu.VMEM(gate_weight.shape, BF16),
             pltpu.VMEM((2, 2, 2, 2, 4, 16, 1024), F32),
             pltpu.VMEM((2, 2, STEPS, 2, 2, 16, 1024), BF16),
             pltpu.VMEM((2, 2, STEPS, 2, 2, 16, 1024), BF16),
             pltpu.VMEM((2, 2, 2, 16, 1024), BF16),
             pltpu.VMEM((2, 2, 2, 16, 1024), BF16),
-            dma((2 * n,)), dma((7,)), dma((7,)),
+            dma((2 * n + 1,)), dma((7,)), dma((7,)),
             dma((4, 4, 2)), dma((4, 4, 2)),
             dma((n, 4)), dma((n, 4)),
             dma((n, 9)), dma((n, 9)),
@@ -418,6 +458,14 @@
         ),
         name="swiglu",
     )(tokens, gate_weight, up_weight, cotangent)
+    return pl.pallas_call(
+        hand_over,
+        out_shape=tuple(jax.ShapeDtypeStruct(a.shape, a.dtype) for a in outs),
+        in_specs=[grid] * len(outs),
+        out_specs=(grid,) * len(outs),
+        scratch_shapes=[*(pltpu.VMEM(a.shape, a.dtype) for a in outs), dma((2 * len(outs),))],
+        name="hand_over",
+    )(*outs)
 
 
 def solution(mesh):

time: 119 us -> 110 us (0.924)
  Pallas kernels: 114 us -> 109 us
  local copies, waits for them, and re-layouts: 4.5 us -> 0 us
    pallas_call x1, Pallas kernels: 114 us -> 107 us  [body(): pl.pallas_call(kernel, out_shape=(tile, jax.ShapeDtypeStruct(tokens.shape...]
    unnamed x10 -> x0, local copies, waits for them, and re-layouts: 4.5 us -> none
    pallas_call x0 -> x1, Pallas kernels: none -> 2.21 us  [body(): pl.pallas_call(hand_over, out_shape=tuple((jax.ShapeDtypeStruct(a.shape,...]
where the time goes in v4:
time: 110 us
  Pallas kernels  109 us (99%)
    pallas_call x1, Pallas kernels, body(): pl.pallas_call(kernel, out_shape=(tile, jax.ShapeDtypeStruct(tokens.shape...  107 us
    pallas_call x1, Pallas kernels, body(): pl.pallas_call(hand_over, out_shape=tuple((jax.ShapeDtypeStruct(a.shape,...  2.21 us

profile of v4, /device:TPU:1, one launch (start us, length us, event | category | flops | bytes accessed | tf_op | source)
XLA Modules:
  0.0 110.0 jit_solution(12856644332551803887)
XLA Ops:
  0.6 107.0 %swiglu.1 = (bf16[256,896]{1,0:T(8,128)(2,1)}, bf16[16,4096]{1,0:T(8,128)(2,1)}, bf16[256,896]{1,0:T(8,128)(2,1)}, bf16[256,896]{1,0:T(8,128)(2,1)}) custom-call(bf16[16,4096]{1,0:T(8,128)(2,1)} %tokens.1, bf16[256,896]{1,0:T(8,128)(2,1)} %gate.1, bf16[256,896]{1,0:T(8,128)(2,1)} %up.1, bf16[256,896]{1,0:T(8,128)(2,1)} %cot_far.1), custom_call_target="tpu_custom_call" | custom-call | tf_op jit(solution)/shard_map/swiglu/pallas_call | solution.py:423
  107.6 2.2 %hand_over.1 = (bf16[256,896]{1,0:T(8,128)(2,1)}, bf16[16,4096]{1,0:T(8,128)(2,1)}, bf16[256,896]{1,0:T(8,128)(2,1)}, bf16[256,896]{1,0:T(8,128)(2,1)}) custom-call(bf16[256,896]{1,0:T(8,128)(2,1)} %get-tuple-element.8.refs_0_, bf16[16,4096]{1,0:T(8,128)(2,1)} %get-tuple-element.9.refs_1_, bf16[256,896]{1,0:T(8,128)(2,1)} %get-tuple-element.10.refs_2_, ...), custom_call_target="tpu_custom_call" | custom-call | tf_op jit(solution)/shard_map/hand_over/pallas_call | solution.py:461

commit v5 on v4

--- a/solution.py
+++ b/solution.py
@@ -76,7 +76,7 @@
         return pl.ds(hs[0], len(hs))
 
     barrier = pltpu.get_barrier_semaphore()
-    peers = [{"y": yp}, {"y": ym}, {"z": zp}, {"z": zm}] + [cube_id(*k) for k in CUBE[1:]]
+    peers = [{"y": yp}, {"y": ym}, {"y": y2}, {"z": zp}, {"z": zm}] + [cube_id(*k) for k in CUBE[1:]]
     for peer in peers:
         pl.semaphore_signal(barrier, inc=1, device_id=peer, device_id_type=MESH)
     cot = cot_here
@@ -262,6 +262,16 @@
         f = go(DW[k].at[ym, upper], RY[k].at[1, upper], ys.at[k, 3], yr.at[k, 3], {"y": ym})
         return a, b, e, f
 
+    def sums_direct(k):
+        weight_grad(k, y2)
+        a = go(DW[k].at[y2, upper], QY[k].at[0], ys.at[k, 0], yr.at[k, 0], {"y": y2})
+        b = go(DW[k].at[y2, lower], QY[k].at[1], ys.at[k, 1], yr.at[k, 1], {"y": y2})
+        weight_grad(k, yp)
+        e = go(DW[k].at[yp], RY[k].at[0], ys.at[k, 2], yr.at[k, 2], {"y": yp})
+        weight_grad(k, ym)
+        f = go(DW[k].at[ym], RY[k].at[1], ys.at[k, 3], yr.at[k, 3], {"y": ym})
+        return a, b, e, f
+
     def sums_on(k, a, b):
         a.wait_recv()
         DW[k][yp, upper] = (DW[k][yp, upper].astype(F32) + QY[k][0].astype(F32)).astype(BF16)
@@ -271,7 +281,7 @@
         f = go(DW[k].at[ym, lower], RY[k].at[1, lower], ys.at[k, 5], yr.at[k, 5], {"y": ym})
         return e, f
 
-    def sums_in(k, copies):
+    def sums_in(k, copies, direct=False):
         at, wide = CHUNKS[k]
         weight_grad(k, y)
         arrived(copies)
@@ -279,6 +289,9 @@
         def step(i, _):
             rows = pl.ds(pl.multiple_of(i * 32, 32), 32)
             total = DW[k][y, rows].astype(F32) + RY[k][0, rows].astype(F32) + RY[k][1, rows].astype(F32)
+            if direct:
+                there = pl.ds(pl.multiple_of(lax.rem(i, 4) * 32, 32), 32)
+                total = total + QY[k][i // 4, there].astype(F32)
             total = total.astype(BF16)
             grad_gate[rows, pl.ds(at, wide)] = total[:, :wide]
             grad_up[rows, pl.ds(at, wide)] = total[:, wide:]
@@ -358,6 +371,7 @@
     near = grads_across(l, (0,))
     passed[p].wait_recv()
     out.append(sums_out(p))
+    z_sum(0, 2)
     far.wait_recv()
     far = pass_on(l, (1,))
     back(1 - xh, 1, most, False)
@@ -367,22 +381,20 @@
     near.wait_recv()
     near = pass_on(l, (0,))
     back(1 - xh, 0, most, False)
-    z_sum(0, 2)
     on.append(sums_on(p, *out[p][:2]))
     z_sum(1, 1)
+    z_sum(0, 3)
     near.wait_recv()
     back(1 - xh, 0, (l,), True)
-    out.append(sums_out(l))
+    out.append(sums_direct(l))
     z_sum(1, 2)
-    z_sum(0, 3)
     for k in range(p):
         sums_in(k, (*out[k][2:], *on[k]))
     z_sum(1, 3)
-    on.append(sums_on(l, *out[l][:2]))
     end0 = z_last(0)
     sums_in(p, (*out[p][2:], *on[p]))
     end1 = z_last(1)
-    sums_in(l, (*out[l][2:], *on[l]))
+    sums_in(l, out[l], True)
     arrived(end0)
     arrived(end1)
     for a in range(2):

time: 110 us -> 110 us (level)
  no operation moved by 1% of the time
where the time goes in v5:
time: 110 us
  Pallas kernels  109 us (99%)
    pallas_call x1, Pallas kernels, body(): pl.pallas_call(kernel, out_shape=(tile, jax.ShapeDtypeStruct(tokens.shape...  107 us
    pallas_call x1, Pallas kernels, body(): pl.pallas_call(hand_over, out_shape=tuple((jax.ShapeDtypeStruct(a.shape,...  2.21 us

profile of v5, /device:TPU:1, one launch (start us, length us, event | category | flops | bytes accessed | tf_op | source)
XLA Modules:
  0.0 109.5 jit_solution(6037161912842869883)
XLA Ops:
  0.6 106.5 %swiglu.1 = (bf16[256,896]{1,0:T(8,128)(2,1)}, bf16[16,4096]{1,0:T(8,128)(2,1)}, bf16[256,896]{1,0:T(8,128)(2,1)}, bf16[256,896]{1,0:T(8,128)(2,1)}) custom-call(bf16[16,4096]{1,0:T(8,128)(2,1)} %tokens.1, bf16[256,896]{1,0:T(8,128)(2,1)} %gate.1, bf16[256,896]{1,0:T(8,128)(2,1)} %up.1, bf16[256,896]{1,0:T(8,128)(2,1)} %cot_far.1), custom_call_target="tpu_custom_call" | custom-call | tf_op jit(solution)/shard_map/swiglu/pallas_call | solution.py:435
  107.2 2.2 %hand_over.1 = (bf16[256,896]{1,0:T(8,128)(2,1)}, bf16[16,4096]{1,0:T(8,128)(2,1)}, bf16[256,896]{1,0:T(8,128)(2,1)}, bf16[256,896]{1,0:T(8,128)(2,1)}) custom-call(bf16[256,896]{1,0:T(8,128)(2,1)} %get-tuple-element.8.refs_0_, bf16[16,4096]{1,0:T(8,128)(2,1)} %get-tuple-element.9.refs_1_, bf16[256,896]{1,0:T(8,128)(2,1)} %get-tuple-element.10.refs_2_, ...), custom_call_target="tpu_custom_call" | custom-call | tf_op jit(solution)/shard_map/hand_over/pallas_call | solution.py:473

commit v6 on v5

--- a/solution.py
+++ b/solution.py
@@ -392,8 +392,8 @@
         sums_in(k, (*out[k][2:], *on[k]))
     z_sum(1, 3)
     end0 = z_last(0)
+    end1 = z_last(1)
     sums_in(p, (*out[p][2:], *on[p]))
-    end1 = z_last(1)
     sums_in(l, out[l], True)
     arrived(end0)
     arrived(end1)

time: 110 us -> 110 us (level)
  no operation moved by 1% of the time
where the time goes in v6:
time: 110 us
  Pallas kernels  109 us (99%)
    pallas_call x1, Pallas kernels, body(): pl.pallas_call(kernel, out_shape=(tile, jax.ShapeDtypeStruct(tokens.shape...  107 us
    pallas_call x1, Pallas kernels, body(): pl.pallas_call(hand_over, out_shape=tuple((jax.ShapeDtypeStruct(a.shape,...  2.21 us

profile of v6, /device:TPU:1, one launch (start us, length us, event | category | flops | bytes accessed | tf_op | source)
XLA Modules:
  0.0 109.5 jit_solution(1451516907269877903)
XLA Ops:
  0.6 106.5 %swiglu.1 = (bf16[256,896]{1,0:T(8,128)(2,1)}, bf16[16,4096]{1,0:T(8,128)(2,1)}, bf16[256,896]{1,0:T(8,128)(2,1)}, bf16[256,896]{1,0:T(8,128)(2,1)}) custom-call(bf16[16,4096]{1,0:T(8,128)(2,1)} %tokens.1, bf16[256,896]{1,0:T(8,128)(2,1)} %gate.1, bf16[256,896]{1,0:T(8,128)(2,1)} %up.1, bf16[256,896]{1,0:T(8,128)(2,1)} %cot_far.1), custom_call_target="tpu_custom_call" | custom-call | tf_op jit(solution)/shard_map/swiglu/pallas_call | solution.py:435
  107.2 2.2 %hand_over.1 = (bf16[256,896]{1,0:T(8,128)(2,1)}, bf16[16,4096]{1,0:T(8,128)(2,1)}, bf16[256,896]{1,0:T(8,128)(2,1)}, bf16[256,896]{1,0:T(8,128)(2,1)}) custom-call(bf16[256,896]{1,0:T(8,128)(2,1)} %get-tuple-element.8.refs_0_, bf16[16,4096]{1,0:T(8,128)(2,1)} %get-tuple-element.9.refs_1_, bf16[256,896]{1,0:T(8,128)(2,1)} %get-tuple-element.10.refs_2_, ...), custom_call_target="tpu_custom_call" | custom-call | tf_op jit(solution)/shard_map/hand_over/pallas_call | solution.py:473
